TPU v7x, 32 devices: a whole 2x2x4 slice. The times are simulated.
32 devices in a mesh: slide: 8 (over z, x), ctx: 4 (over y, core).
Axes of the slice: x: 2, y: 2, z: 4, core: 2. Of those that a mesh axis runs over, the one named last changes fastest.
Arguments:
- feature_maps: bfloat16 [1024, 16, 16, 384], P(('slide', 'ctx')), may hold values from -6 to 6
- down_weight: bfloat16 [1536, 768], replicated, may hold values from -0.15625 to 0.15625
- conv_taps: bfloat16 [49, 768], replicated, may hold values from -0.875 to 0.875
- mlp_in: bfloat16 [768, 3072], replicated, may hold values from -0.21875 to 0.21875
- mlp_out: bfloat16 [3072, 768], replicated, may hold values from -0.109375 to 0.109375
- layer_scale: float32 [768], replicated, may hold values from 0.2 to 1
- qkv_weight: bfloat16 [1, 768, 2304], replicated, may hold values from -4.690971 to 4.690971
- out_weight: bfloat16 [1, 768, 768], replicated, may hold values from -0.21875 to 0.21875
- tile_slide: int32 [1024], P(('slide', 'ctx')), may hold values from 0 to 7, as said below
- tile_pos: int32 [1024], P(('slide', 'ctx')), may hold values from 0 to 767, as said below
- slide_len: int32 [8], replicated, may hold values from 1 to 768, as said below
Outputs:
- slide_tokens: bfloat16 [6144, 768], P(('slide', 'ctx'))
Inputs may be any that keep to these rules, and one draw needn't show every extreme that they name: `tile_slide`: the tiles of slide s lie at positions 0 to slide_len[s] - 1 of it, exactly one tile at each. `tile_pos`: among the tiles of one device at most 6 lie in the same block of 192 positions of one slide, and some device has exactly 6 in some block. `slide_len`: the lengths sum to 1024; some slide has exactly 768 tiles.
All inputs are finite; a program needn't handle non-finite values.
Results may differ from a plain program's by a relative error of at most 0.015.
Values may be sent and summed in bfloat16 or wider, within the bound.
No kernel may reach another device: no remote copies, remote signals or barrier semaphores. Data moves between devices by JAX's collectives and lax.ppermute only.
A program may use at most 128 MiB of HBM per device.

v0:
```python
import jax
import jax.numpy as jnp
from jax import lax
from jax.sharding import PartitionSpec as P

HEADS = 12
HEAD_DIM = 64
KS = 7
SEQ_DEV = 192


NORM_EPS = 1e-06
FAR_NEGATIVE = -1e30


def layer_norm(values):
    center = values - jnp.mean(values, axis=-1, keepdims=True)
    spread = jnp.mean(center * center, axis=-1, keepdims=True)
    return center * lax.rsqrt(spread + NORM_EPS)


def encode_tiles(tile_maps, down_weight, conv_taps, mlp_in, mlp_out, layer_scale):
    tile_count = tile_maps.shape[0]
    half_side = tile_maps.shape[1] // 2
    chan_count = tile_maps.shape[3]
    model_width = down_weight.shape[1]
    normed = layer_norm(tile_maps.astype(jnp.float32)).astype(jnp.bfloat16)
    patches = normed.reshape(tile_count, half_side, 2, half_side, 2, chan_count).transpose(
        0, 1, 3, 2, 4, 5
    )
    patches = patches.reshape(tile_count * half_side * half_side, 4 * chan_count)
    reduced = jnp.dot(patches, down_weight, preferred_element_type=jnp.float32).astype(jnp.bfloat16)
    widened = reduced.reshape(tile_count, half_side, half_side, model_width).astype(jnp.float32)
    tap_values = conv_taps.astype(jnp.float32)
    pad_reach = KS // 2
    padded = jnp.pad(widened, ((0, 0), (pad_reach, pad_reach), (pad_reach, pad_reach), (0, 0)))
    spatial = jnp.zeros_like(widened)
    for row_off in range(KS):
        for col_off in range(KS):
            spatial = (
                spatial
                + padded[:, row_off : row_off + half_side, col_off : col_off + half_side, :]
                * tap_values[row_off * KS + col_off]
            )
    spatial_normed = (
        layer_norm(spatial)
        .astype(jnp.bfloat16)
        .reshape(tile_count * half_side * half_side, model_width)
    )
    expanded = jax.nn.gelu(
        jnp.dot(spatial_normed, mlp_in, preferred_element_type=jnp.float32), approximate=False
    ).astype(jnp.bfloat16)
    branch = jnp.dot(expanded, mlp_out, preferred_element_type=jnp.float32)
    blocked = widened + (layer_scale * branch).reshape(
        tile_count, half_side, half_side, model_width
    )
    pooled = jnp.mean(blocked, axis=(1, 2))
    return layer_norm(pooled).astype(jnp.bfloat16)


def shards(
    feature_maps,
    down_weight,
    conv_taps,
    mlp_in,
    mlp_out,
    layer_scale,
    qkv_weight,
    out_weight,
    tile_slide,
    tile_pos,
    slide_len,
):
    slide_count = lax.axis_size("slide")
    ctx_count = lax.axis_size("ctx")
    device_count = slide_count * ctx_count
    capacity = (SEQ_DEV + device_count - 1) // device_count
    buffer_rows = device_count * capacity
    model_width = qkv_weight.shape[1]
    tiles_here = feature_maps.shape[0]
    embeds = encode_tiles(feature_maps, down_weight, conv_taps, mlp_in, mlp_out, layer_scale)
    owner_index = tile_slide * ctx_count + tile_pos // SEQ_DEV
    tile_order = jnp.arange(tiles_here, dtype=jnp.int32)
    earlier = (owner_index[None, :] == owner_index[:, None]) & (
        tile_order[None, :] < tile_order[:, None]
    )
    tile_rank = jnp.sum(earlier.astype(jnp.int32), axis=1)
    target_row = owner_index * capacity + tile_rank
    placing = jnp.arange(buffer_rows, dtype=jnp.int32)[:, None] == target_row[None, :]
    outgoing = jnp.dot(
        placing.astype(jnp.bfloat16), embeds, preferred_element_type=jnp.float32
    ).astype(jnp.bfloat16)
    local_slot = tile_pos % SEQ_DEV
    slot_sent = jnp.sum(jnp.where(placing, local_slot[None, :] + 1, 0), axis=1) - 1
    slot_sent = jnp.where(slot_sent < 0, SEQ_DEV, slot_sent)
    arrived, arrived_slot = (
        lax.all_to_all(outgoing, ("slide", "ctx"), split_axis=0, concat_axis=0, tiled=True),
        lax.all_to_all(slot_sent, ("slide", "ctx"), split_axis=0, concat_axis=0, tiled=True),
    )
    position = jnp.arange(SEQ_DEV, dtype=jnp.int32)
    picking = (position[:, None] == arrived_slot[None, :]).astype(jnp.bfloat16)
    slot_rows = jnp.dot(picking, arrived, preferred_element_type=jnp.float32).astype(jnp.bfloat16)
    stream = slot_rows.astype(jnp.float32)
    length = slide_len[lax.axis_index("slide")]
    query_pos = lax.axis_index("ctx") * SEQ_DEV + position
    score_scale = HEAD_DIM ** (-0.5)
    lnorm = layer_norm(stream).astype(jnp.bfloat16)
    query_weight = qkv_weight[0, :, :model_width]
    key_weight = qkv_weight[0, :, model_width:]
    queries = jnp.dot(lnorm, query_weight, preferred_element_type=jnp.float32).astype(jnp.bfloat16)
    queries = queries.reshape(SEQ_DEV, HEADS, HEAD_DIM)
    local_kv = jnp.dot(lnorm, key_weight, preferred_element_type=jnp.float32).astype(jnp.bfloat16)
    key_rows = lax.all_gather(local_kv, "ctx", axis=0, tiled=True)
    running_max = jnp.full((HEADS, SEQ_DEV), FAR_NEGATIVE, jnp.float32)
    row_count = key_rows.shape[0]
    keys_part = key_rows[:, :model_width].reshape(row_count, HEADS, HEAD_DIM)
    values_part = key_rows[:, model_width:].reshape(row_count, HEADS, HEAD_DIM)
    scores = (
        jnp.einsum("qhe,khe->hqk", queries, keys_part, preferred_element_type=jnp.float32)
        * score_scale
    )
    included = jnp.arange(row_count, dtype=jnp.int32) < length
    scores = jnp.where(included[None, None, :], scores, FAR_NEGATIVE)
    new_max = jnp.maximum(running_max, jnp.max(scores, axis=-1))
    weights = jnp.where(included[None, None, :], jnp.exp(scores - new_max[:, :, None]), 0.0)
    denom_sum = jnp.sum(weights, axis=-1)
    accum = jnp.einsum(
        "hqk,khe->hqe",
        weights.astype(jnp.bfloat16),
        values_part,
        preferred_element_type=jnp.float32,
    )
    folded = (new_max, denom_sum, accum)
    running_max, denom_sum, accum = folded
    attended = (accum / denom_sum[:, :, None]).transpose(1, 0, 2).reshape(SEQ_DEV, model_width)
    attended = attended.astype(jnp.bfloat16)
    stream = stream + jnp.dot(attended, out_weight[0], preferred_element_type=jnp.float32)
    valid_rows = query_pos < length
    return jnp.where(valid_rows[:, None], stream, 0.0).astype(jnp.bfloat16)


def solution(mesh):
    return jax.shard_map(
        shards,
        mesh=mesh,
        in_specs=(
            P(("slide", "ctx"), None, None, None),
            P(),
            P(),
            P(),
            P(),
            P(),
            P(),
            P(),
            P(("slide", "ctx")),
            P(("slide", "ctx")),
            P(),
        ),
        out_specs=P(("slide", "ctx"), None),
        check_vma=False,
    )
```

profile of v0, /device:TPU:0, one launch (start us, length us, event | category | flops | bytes accessed | tf_op | source)
XLA Modules:
  0.0 350.1 jit_solution(11754218839392690077)
XLA Ops:
  6.5 0.8 fusion.146
  7.4 0.2 convert_reduce_fusion.1
  7.7 0.5 copy-done.8
  8.2 0.6 compare_select_fusion
  8.9 7.4 %all-to-all-start = ((s32[32,6,1]{1,2,0:T(1,128)}), s32[32,6,1]{1,2,0:T(1,128)}, u32[]{:S(2)}, u32[]{:S(2)}) async-start(s32[32,6,1]{1,2,0:T(1,128)} %bitcast.1), calls=%async_computation | async-start | bytes 32768 | tf_op jit(solution)/shard_map/all_to_all | solution.py:98
  16.3 1.1 convert_element_type.70
  17.4 0.2 slice_reduce_fusion.48
  17.8 4.3 %convert_reduce_fusion = f32[32,16,16]{2,1,0:T(8,128)S(1)} fusion(bf16[32,16,16,384]{3,2,1,0:T(8,128)(2,1)} %param.11), kind=kLoop, calls=%fused_computation.68 | loop fusion | flops 6283264 | bytes 6324224 | tf_op jit(solution)/shard_map/reduce_sum | solution.py:17
  22.1 3.1 fusion.12
  25.3 4.3 %fusion.13 = bf16[32,16,16,384]{3,2,1,0:T(8,128)(2,1)} fusion(bf16[32,16,16,384]{3,2,1,0:T(8,128)(2,1)S(1)} %copy-done.2, f32[32,16,16]{2,1,0:T(8,128)S(1)} %add_rsqrt_fusion, f32[32,16,16]{2,1,0:T(8,128)S(1)} %broadcast_multiply_fusion), kind=kLoop, calls=%fused_computation.72 | loop fusion | flops 12582912 | bytes 12648448 | tf_op jit(solution)/shard_map/convert_element_type | solution.py:27
  29.6 13.3 %reshape.166 = bf16[32,8,2,8,2,384]{5,4,3,2,1,0:T(2,128)(2,1)} reshape(bf16[32,16,16,384]{3,2,1,0:T(8,128)(2,1)} %fusion.13) | data formatting | bytes 12582912 | tf_op jit(solution)/shard_map/reshape | solution.py:28
  42.9 6.9 %copy.30 = bf16[32,8,2,8,2,384]{5,4,2,3,1,0:T(2,128)(2,1)} copy(bf16[32,8,2,8,2,384]{5,4,3,2,1,0:T(2,128)(2,1)} %reshape.166) | data formatting | bytes 12582912 | tf_op jit(solution)/shard_map/reshape | solution.py:28
  49.8 14.4 %reshape.167 = bf16[2048,1536]{1,0:T(8,128)(2,1)} reshape(bf16[32,8,8,2,2,384]{5,4,3,2,1,0:T(2,128)(2,1)} %bitcast.55) | data formatting | bytes 12582912 | tf_op jit(solution)/shard_map/reshape | solution.py:31
  64.2 8.2 %convolution_convert_fusion = bf16[2048,768]{1,0:T(8,128)(2,1)S(1)} fusion(bf16[2048,1536]{1,0:T(8,128)(2,1)} %reshape.167, bf16[1536,768]{1,0:T(8,128)(2,1)S(1)} %copy-done), kind=kOutput, calls=%fused_computation.183 | convolution fusion | flops 4833411072 | bytes 11796480 | tf_op jit(solution)/shard_map/dot_general | solution.py:32
  72.4 1.7 copy-done.5
  74.1 3.4 bitcast_convert_fusion
  77.5 120.8 %fusion.184 = (f32[32,8,8]{2,1,0:T(8,128)S(1)}, f32[32,8,8,768]{3,2,1,0:T(8,128)}) fusion(f32[768]{0:T(1024)S(1)} %get-tuple-element.6, f32[768]{0:T(1024)S(1)} %get-tuple-element.7, f32[768]{0:T(1024)S(1)} %get-tuple-element.8, f32[768]{0:T(1024)S(1)} %get-tuple-element.9, f32[768]{0:T(1024)S(1)} %get-tuple-element.10, f32[768]{0:T(1024)S(1)} %get-tuple-element.11, ...), kind=kLoop, calls=%fused_computation.317 | loop fusion | flops 154138624 | bytes 12741632 | tf_op jit(solution)/shard_map/reduce_sum | solution.py:17
  198.4 3.7 %multiply_reduce_fusion = f32[32,8,8]{2,1,0:T(8,128)S(1)} fusion(f32[32,8,8,768]{3,2,1,0:T(8,128)} %get-tuple-element.55, f32[32,8,8]{2,1,0:T(8,128)S(1)} %broadcast_multiply_fusion.1), kind=kLoop, calls=%fused_computation.176 | loop fusion | flops 4716544 | bytes 6307840 | tf_op jit(solution)/shard_map/reduce_sum | solution.py:18
  202.2 0.8 copy-done.3
  203.0 0.8 multiply_convert_fusion
  203.8 0.8 slice-done
  204.6 62.4 %fusion.207 = bf16[2048,3072]{1,0:T(8,128)(2,1)S(1)} fusion(bf16[2048,768]{1,0:T(8,128)(2,1)S(1)} %bitcast.57, bf16[768,3072]{1,0:T(8,128)(2,1)S(1)} %bitcast.63), kind=kOutput, calls=%fused_computation.51.clone.clone.clone.clone.clone.clone.1 | convolution fusion | flops 10072621056 | bytes 20447232 | tf_op jit(solution)/shard_map/dot_general | solution.py:51
  267.0 10.2 %add_reduce_fusion = f32[32,768]{1,0:T(8,128)S(1)} fusion(bf16[2048,768]{1,0:T(8,128)(2,1)S(1)} %copy-done.6, bf16[3072,768]{1,0:T(8,128)(2,1)S(1)} %copy-done.10, f32[768]{0:T(1024)S(1)} %copy-done.11, bf16[2048,3072]{1,0:T(8,128)(2,1)S(1)} %fusion.207), kind=kOutput, calls=%fused_computation.174 | convolution fusion | flops 9669943296 | bytes 20548608 | tf_op jit(solution)/shard_map/dot_general | solution.py:53
  277.4 0.2 multiply_reduce_fusion.2
  277.6 0.4 convolution_convert_fusion.2
  278.0 0.8 all_to_all.13
  278.8 5.8 %all-to-all-start.1 = ((bf16[32,6,768]{2,1,0:T(8,128)(2,1)}), bf16[32,6,768]{2,1,0:T(8,128)(2,1)S(1)}, u32[]{:S(2)}, u32[]{:S(2)}) async-start(bf16[32,6,768]{2,1,0:T(8,128)(2,1)} %all_to_all.13), calls=%async_computation.1 | async-start | bytes 786432 | tf_op jit(solution)/shard_map/all_to_all | solution.py:97
  284.6 0.3 all-gather.2.cloned.1.call-start
  284.8 0.5 broadcast.215
  285.4 1.4 reduce.101
  286.9 10.9 %all-to-all-done.1 = bf16[32,6,768]{2,1,0:T(8,128)(2,1)S(1)} async-done(((bf16[32,6,768]{2,1,0:T(8,128)(2,1)}), bf16[32,6,768]{2,1,0:T(8,128)(2,1)S(1)}, u32[]{:S(2)}, u32[]{:S(2)}) %all-to-all-start.1) | async-done | bytes 294944 | tf_op jit(solution)/shard_map/all_to_all | solution.py:97
  297.9 0.3 fusion.187
  298.2 0.2 multiply_reduce_fusion.1
  298.4 3.2 convolution_convert_fusion.1
  301.6 0.6 dynamic_slice.3
  302.2 0.7 add_compare_fusion
  302.9 0.7 iota_compare_fusion.5
  303.5 1.7 convolution_convert_fusion.3
  305.3 0.2 copy.26
  305.4 18.4 %all-gather.2.cloned.1.call-done = bf16[768,1536]{1,0:T(8,128)(2,1)} async-done(((bf16[192,1536]{1,0:T(8,128)(2,1)}), bf16[768,1536]{1,0:T(8,128)(2,1)}) %all-gather.2.cloned.1.call-update) | async-done | bytes 2359312 | tf_op jit(solution)/shard_map/all_gather | solution.py:113
  323.9 2.8 fusion.186
  326.7 1.6 copy.27
  328.3 4.1 %fusion.114 = (f32[12,192]{1,0:T(8,128)S(1)}, f32[12,192,768]{2,1,0:T(8,128)}) fusion(pred[768]{0:T(1024)(128)(4,1)S(1)} %iota_compare_fusion.5, bf16[192,12,64]{0,2,1:T(8,128)(2,1)S(1)} %bitcast.58, bf16[768,12,64]{0,2,1:T(8,128)(2,1)S(1)} %bitcast.56), kind=kOutput, calls=%fused_computation.177 | convolution fusion | flops 231798528 | bytes 8562432 | tf_op jit(solution)/shard_map/qhe,khe->hqk/dot_general | solution.py:119
  332.3 1.4 copy.28
  333.8 4.6 %fusion.115 = f32[12,192]{1,0:T(8,128)S(1)} fusion(f32[12,192,768]{2,1,0:T(8,128)} %get-tuple-element.63, f32[12,192]{1,0:T(8,128)S(1)} %broadcast_maximum_fusion, pred[768]{0:T(1024)(128)(4,1)S(1)} %iota_compare_fusion.5), kind=kLoop, calls=%fused_computation.178 | loop fusion | flops 8845056 | bytes 7097088 | tf_op jit(solution)/shard_map/reduce_sum | solution.py:126
  338.4 0.5 copy-done.4
  338.9 3.3 fusion.137
  342.1 1.1 fusion.130
  (46 shorter events, 1.0 us)
Async XLA Ops:
  6.5 57.7 %copy-start = (bf16[1536,768]{1,0:T(8,128)(2,1)S(1)}, bf16[1536,768]{1,0:T(8,128)(2,1)}, u32[]{:S(2)}) copy-start(bf16[1536,768]{1,0:T(8,128)(2,1)} %param.12) | copy-start | bytes 7077892
  7.6 0.6 copy-start.8
  8.9 269.9 %all-to-all-start = ((s32[32,6,1]{1,2,0:T(1,128)}), s32[32,6,1]{1,2,0:T(1,128)}, u32[]{:S(2)}, u32[]{:S(2)}) async-start(s32[32,6,1]{1,2,0:T(1,128)} %bitcast.1), calls=%async_computation | async-start | bytes 32768 | tf_op jit(solution)/shard_map/all_to_all | solution.py:98
  16.3 5.8 %copy-start.2 = (bf16[32,16,16,384]{3,2,1,0:T(8,128)(2,1)S(1)}, bf16[32,16,16,384]{3,2,1,0:T(8,128)(2,1)}, u32[]{:S(2)}) copy-start(bf16[32,16,16,384]{3,2,1,0:T(8,128)(2,1)} %param.11) | copy-start | bytes 18874372
  72.4 1.7 copy-start.5
  198.4 4.6 %copy-start.3 = (f32[32,8,8,768]{3,2,1,0:T(8,128)S(1)}, f32[32,8,8,768]{3,2,1,0:T(8,128)}, u32[]{:S(2)}) copy-start(f32[32,8,8,768]{3,2,1,0:T(8,128)} %get-tuple-element.55) | copy-start | bytes 18874372
  202.1 2.4 slice-start
  203.0 1.6 slice-start.1
  204.6 62.4 %copy-start.6 = (bf16[2048,768]{1,0:T(8,128)(2,1)S(1)}, bf16[2048,768]{1,0:T(8,128)(2,1)}, u32[]{:S(2)}) copy-start(bf16[2048,768]{1,0:T(8,128)(2,1)} %copy-done.5) | copy-start | bytes 9437188
  204.6 62.4 %copy-start.10 = (bf16[3072,768]{1,0:T(8,128)(2,1)S(1)}, bf16[3072,768]{1,0:T(8,128)(2,1)}, u32[]{:S(2)}) copy-start(bf16[3072,768]{1,0:T(8,128)(2,1)} %param.15) | copy-start | bytes 14155780
  204.6 62.4 %copy-start.11 = (f32[768]{0:T(1024)S(1)}, f32[768]{0:T(1024)}, u32[]{:S(2)}) copy-start(f32[768]{0:T(1024)} %param.16) | copy-start | bytes 9220
  267.0 10.6 %copy-start.9 = (s32[32]{0:T(128)S(1)}, s32[32]{0:T(128)}, u32[]{:S(2)}) copy-start(s32[32]{0:T(128)} %copy-done.8) | copy-start | bytes 388
  277.3 24.4 %copy-start.12 = (s32[8]{0:T(128)S(1)}, s32[8]{0:T(128)}, u32[]{:S(2)}) copy-start(s32[8]{0:T(128)} %param.21) | copy-start | bytes 100
  278.8 18.9 %all-to-all-start.1 = ((bf16[32,6,768]{2,1,0:T(8,128)(2,1)}), bf16[32,6,768]{2,1,0:T(8,128)(2,1)S(1)}, u32[]{:S(2)}, u32[]{:S(2)}) async-start(bf16[32,6,768]{2,1,0:T(8,128)(2,1)} %all_to_all.13), calls=%async_computation.1 | async-start | bytes 786432 | tf_op jit(solution)/shard_map/all_to_all | solution.py:97
  284.6 39.3 %all-gather.2.cloned.1.call-start = ((), (), s32[]{:S(2)}) async-start(), calls=%async_computation.2 | async-start | bytes 2949120 | tf_op jit(solution)/shard_map/all_gather | solution.py:113
  333.8 5.1 %copy-start.4 = (f32[12,192,768]{2,1,0:T(8,128)S(1)}, f32[12,192,768]{2,1,0:T(8,128)}, u32[]{:S(2)}) copy-start(f32[12,192,768]{2,1,0:T(8,128)} %get-tuple-element.63) | copy-start | bytes 21233668
  338.4 4.9 %copy-start.1 = (bf16[1536,768]{1,0:T(8,128)(2,1)S(1)}, bf16[1536,768]{1,0:T(8,128)(2,1)}, u32[]{:S(2)}) copy-start(bf16[1536,768]{1,0:T(8,128)(2,1)} %param.12) | copy-start | bytes 7077892
  338.9 3.3 copy-start.7
Sparse Core Ops, SparseCore 0:
  301.7 22.0 all-gather.1
where the time goes:
time: 351 us; the launch traced here: 350 us
  other arithmetic  151 us (43%)
  matrix products  94.9 us (27%)
  local copies, waits for them, and re-layouts  47.5 us (14%)
  waiting for transfers between devices  29.3 us (8%)
  between operations  13.7 us (4%)
  starting transfers between devices  13.4 us (4%)
    reduce_sum x3, other arithmetic, layer_norm(): center = values - jnp.mean(values, axis=-1, keepdims=True)  125 us
    dot_general x1, matrix products, encode_tiles(): jnp.dot(spatial_normed, mlp_in, preferred_element_type=jnp.float32)  62.4 us
    reshape x2, local copies, waits for them, and re-layouts, encode_tiles(): normed.reshape(tile_count, half_side, 2, half_side, 2, chan_count)  20.1 us
    all_gather x1, waiting for transfers between devices, shards(): key_rows = lax.all_gather(local_kv, 'ctx', axis=0, tiled=True)  18.4 us
    reshape x1, local copies, waits for them, and re-layouts, encode_tiles(): patches.reshape(tile_count * half_side * half_side, 4 * chan_count)  14.4 us
    all_to_all x1, waiting for transfers between devices, shards(): lax.all_to_all(outgoing, ('slide', 'ctx'), split_axis=0, concat_axis=0, t...  10.9 us
    dot_general x1, matrix products, encode_tiles(): branch = jnp.dot(expanded, mlp_out, preferred_element_type=jnp.float32)  10.2 us
    dot_general x1, matrix products, encode_tiles(): jnp.dot(patches, down_weight, preferred_element_type=jnp.float32)  8.21 us
  transfers between devices with their start and end apart: 3, of which 2 were waited for; matrix products, arithmetic and copies ran while one was open for 75% of the time, Pallas kernels for 0%

commit v1 on v0

--- a/solution.py
+++ b/solution.py
@@ -1,6 +1,11 @@
+import functools
+
 import jax
 import jax.numpy as jnp
+import numpy as np
 from jax import lax
+from jax.experimental import pallas as pl
+from jax.experimental.pallas import tpu as pltpu
 from jax.sharding import PartitionSpec as P
 
 HEADS = 12
@@ -19,43 +24,96 @@
     return center * lax.rsqrt(spread + NORM_EPS)
 
 
-def encode_tiles(tile_maps, down_weight, conv_taps, mlp_in, mlp_out, layer_scale):
-    tile_count = tile_maps.shape[0]
-    half_side = tile_maps.shape[1] // 2
-    chan_count = tile_maps.shape[3]
-    model_width = down_weight.shape[1]
-    normed = layer_norm(tile_maps.astype(jnp.float32)).astype(jnp.bfloat16)
-    patches = normed.reshape(tile_count, half_side, 2, half_side, 2, chan_count).transpose(
-        0, 1, 3, 2, 4, 5
-    )
-    patches = patches.reshape(tile_count * half_side * half_side, 4 * chan_count)
-    reduced = jnp.dot(patches, down_weight, preferred_element_type=jnp.float32).astype(jnp.bfloat16)
-    widened = reduced.reshape(tile_count, half_side, half_side, model_width).astype(jnp.float32)
-    tap_values = conv_taps.astype(jnp.float32)
-    pad_reach = KS // 2
-    padded = jnp.pad(widened, ((0, 0), (pad_reach, pad_reach), (pad_reach, pad_reach), (0, 0)))
-    spatial = jnp.zeros_like(widened)
-    for row_off in range(KS):
-        for col_off in range(KS):
-            spatial = (
-                spatial
-                + padded[:, row_off : row_off + half_side, col_off : col_off + half_side, :]
-                * tap_values[row_off * KS + col_off]
-            )
-    spatial_normed = (
-        layer_norm(spatial)
-        .astype(jnp.bfloat16)
-        .reshape(tile_count * half_side * half_side, model_width)
-    )
-    expanded = jax.nn.gelu(
-        jnp.dot(spatial_normed, mlp_in, preferred_element_type=jnp.float32), approximate=False
-    ).astype(jnp.bfloat16)
-    branch = jnp.dot(expanded, mlp_out, preferred_element_type=jnp.float32)
-    blocked = widened + (layer_scale * branch).reshape(
-        tile_count, half_side, half_side, model_width
-    )
-    pooled = jnp.mean(blocked, axis=(1, 2))
-    return layer_norm(pooled).astype(jnp.bfloat16)
+F32=jnp.float32; BF=jnp.bfloat16
+FREQ=64
+
+def tables(side, ks):
+    reach=ks//2; n=side+reach
+    half=[(0,0)]+[(0,l) for l in range(1,n//2+1)]+[(k,l) for k in range(1,n//2+1) for l in range(n)]
+    k=np.array([a for a,_ in half]); l=np.array([b for _,b in half])
+    pos=np.arange(side*side); i,j=pos//side,pos%side
+    th=2*np.pi*(np.outer(k,i)+np.outer(l,j))/n
+    fwd=np.zeros((2*FREQ,side*side)); fwd[:len(half)]=np.cos(th); fwd[FREQ:FREQ+len(half)]=-np.sin(th)
+    a=np.arange(ks*ks)//ks-reach; b=np.arange(ks*ks)%ks-reach
+    ph=2*np.pi*(np.outer(k,a)+np.outer(l,b))/n
+    s=np.where(np.arange(len(half))==0,1.0,2.0)[:,None]/(n*n)
+    tap=np.zeros((2*FREQ,ks*ks)); tap[:len(half)]=s*np.cos(ph); tap[FREQ:FREQ+len(half)]=s*np.sin(ph)
+    inv=fwd.T.copy()
+    perm=np.zeros((4*side*side,4*side*side))
+    for dy in range(2):
+        for dx in range(2):
+            for ii in range(side):
+                for jj in range(side):
+                    perm[(dy*2+dx)*side*side+ii*side+jj,(2*ii+dy)*2*side+2*jj+dx]=1
+    hi=tap.astype(jnp.bfloat16).astype(np.float64)
+    return fwd, inv, np.concatenate([hi,tap-hi]), perm
+
+def rows_norm(x):
+    c=x-jnp.mean(x,axis=-1,keepdims=True)
+    return c*lax.rsqrt(jnp.mean(c*c,axis=-1,keepdims=True)+NORM_EPS)
+
+def gelu_sum_part(h):
+    w=jnp.minimum(h*h, 50.0)
+    p=0.7975009723173133+w*(0.03701192786292476-0.000352536613169665*w)
+    hv=0.5*h
+    return hv+hv*jnp.tanh(h*p)
+
+def kernel(G, side, feat, down, taps, win, wout, scale, fwd, inv, taptab, perm, out,
+           patches, red, sn, psum, pool, khat):
+    step=pl.program_id(0); steps=pl.num_programs(0)
+    S=side*side
+    C=feat.shape[-1]; D=down.shape[1]; M=win.shape[1]
+    @pl.when(step==0)
+    def _():
+        t2=jnp.dot(taptab[...],taps[...],preferred_element_type=F32)
+        khat[...]=t2[:2*FREQ]+t2[2*FREQ:]
+    @pl.loop(0,G)
+    def _(t):
+        xp=jnp.dot(perm[...],feat[t],preferred_element_type=F32)
+        n=rows_norm(xp).astype(BF)
+        for q in range(4):
+            patches[pl.ds(pl.multiple_of(t*S,S),S), q*C:(q+1)*C]=n[q*S:(q+1)*S]
+    red[...]=jnp.dot(patches[...],down[...],preferred_element_type=F32).astype(BF)
+    @pl.loop(0,G)
+    def _(t):
+        rows=pl.ds(pl.multiple_of(t*S,S),S)
+        f=jnp.dot(fwd[...],red[rows,:],preferred_element_type=F32)
+        pool[pl.ds(step*G+t,1),:]=f[0:1]*(1.0/S)
+        fr,fi=f[:FREQ],f[FREQ:]
+        kr,ki=khat[:FREQ,:],khat[FREQ:,:]
+        g=jnp.concatenate([fr*kr-fi*ki, fr*ki+fi*kr],axis=0).astype(BF)
+        sp=jnp.dot(inv[...],g,preferred_element_type=F32)
+        sn[rows,:]=rows_norm(sp).astype(BF)
+    NC=256
+    for c in range(M//NC):
+        h=jnp.dot(sn[...],win[:,c*NC:(c+1)*NC],preferred_element_type=F32)
+        e=gelu_sum_part(h)
+        e=e.reshape(G,S//8,8,NC).sum(axis=1).reshape(G*8,NC)
+        psum[pl.ds(pl.multiple_of(step*G*8,G*8),G*8), c*NC:(c+1)*NC]=e.astype(BF)
+    @pl.when(step==steps-1)
+    def _():
+        z=jnp.dot(psum[...],wout[...],preferred_element_type=F32)
+        z=z.reshape(z.shape[0]//8,8,D).sum(axis=1)*(1.0/S)
+        out[...]=rows_norm(pool[...]+scale[...]*z).astype(BF)
+
+def encode(feature_maps, down, taps, win, wout, scale, G=8):
+    T,H,W,C=feature_maps.shape
+    side=H//2; S=side*side; D=down.shape[1]; M=win.shape[1]; ks=int(round(taps.shape[0]**.5))
+    fwd,inv,tt,perm=tables(side,ks)
+    args=(feature_maps.reshape(T,H*W,C),down,taps,win,wout,scale.reshape(1,D),
+          jnp.asarray(fwd,BF),jnp.asarray(inv,BF),jnp.asarray(tt,BF),jnp.asarray(perm,BF))
+    full=lambda a: pl.BlockSpec(a.shape,lambda s:(0,)*a.ndim,pipeline_mode=pl.Buffered(1))
+    return pl.pallas_call(
+        functools.partial(kernel,G,side),
+        grid=(T//G,),
+        in_specs=[pl.BlockSpec((G,H*W,C),lambda s:(s,0,0))]+[full(a) for a in args[1:]],
+        out_specs=pl.BlockSpec((T,D),lambda s:(0,0)),
+        out_shape=jax.ShapeDtypeStruct((T,D),BF),
+        scratch_shapes=[pltpu.VMEM((G*S,4*C),BF),pltpu.VMEM((G*S,D),BF),pltpu.VMEM((G*S,D),BF),
+                        pltpu.VMEM((T*8,M),BF),pltpu.VMEM((T,D),F32),pltpu.VMEM((2*FREQ,D),F32)],
+        compiler_params=pltpu.CompilerParams(vmem_limit_bytes=60*1024*1024, dimension_semantics=("arbitrary",)),
+        name="encode",
+    )(*args)
 
 
 def shards(
@@ -78,7 +136,7 @@
     buffer_rows = device_count * capacity
     model_width = qkv_weight.shape[1]
     tiles_here = feature_maps.shape[0]
-    embeds = encode_tiles(feature_maps, down_weight, conv_taps, mlp_in, mlp_out, layer_scale)
+    embeds = encode(feature_maps, down_weight, conv_taps, mlp_in, mlp_out, layer_scale)
     owner_index = tile_slide * ctx_count + tile_pos // SEQ_DEV
     tile_order = jnp.arange(tiles_here, dtype=jnp.int32)
     earlier = (owner_index[None, :] == owner_index[:, None]) & (

time: 351 us -> 145 us (0.41)
  other arithmetic: 151 us -> 5.87 us
  matrix products: 94.9 us -> 10.8 us
  Pallas kernels: 0 us -> 59.7 us
  local copies, waits for them, and re-layouts: 47.5 us -> 10.8 us
    reduce_sum x3 -> x0, other arithmetic: 125 us -> none  [layer_norm(): center = values - jnp.mean(values, axis=-1, keepdims=True)]
    dot_general x3 -> x0, matrix products: 80.8 us -> none  [the longest x1 62.4 us: encode_tiles(): jnp.dot(spatial_normed, mlp_in, preferred_element_type=jnp.float32)]
    pallas_call x0 -> x1, Pallas kernels: none -> 59.7 us  [encode(): pl.pallas_call(functools.partial(kernel, G, side), grid=(T // G,), in_spe...]
    reshape x3 -> x1, local copies, waits for them, and re-layouts: 34.6 us -> 1.28 us  [encode(): scale.reshape(1, D)]
    convert_element_type x4 -> x0, other arithmetic: 9.55 us -> none  [the longest x1 4.28 us: encode_tiles(): normed = layer_norm(tile_maps.astype(jnp.float32)).astype(jnp.bfloat16)]
    reduce_sum x4 -> x1, other arithmetic: 7.26 us -> 0.22 us  [layer_norm(): spread = jnp.mean(center * center, axis=-1, keepdims=True)]
    unnamed x30 -> x6, local copies, waits for them, and re-layouts: 4.3 us -> 0.01 us
  transfers between devices with their start and end apart: 3 -> 3, of which waited for: 2 -> 2; matrix products, arithmetic and copies ran while one was open for 75% -> 5% of each run, Pallas kernels for 0% -> 41%
where the time goes in v1:
time: 145 us; the launch traced here: 144 us
  Pallas kernels  59.7 us (41%)
  waiting for transfers between devices  30.1 us (21%)
  between operations  13.6 us (9%)
  starting transfers between devices  13.4 us (9%)
  local copies, waits for them, and re-layouts  10.8 us (7%)
  matrix products  10.8 us (7%)
  other arithmetic  5.87 us (4%)
    pallas_call x1, Pallas kernels, encode(): pl.pallas_call(functools.partial(kernel, G, side), grid=(T // G,), in_spe...  59.7 us
    all_gather x1, waiting for transfers between devices, shards(): key_rows = lax.all_gather(local_kv, 'ctx', axis=0, tiled=True)  18.4 us
    all_to_all x1, waiting for transfers between devices, shards(): lax.all_to_all(outgoing, ('slide', 'ctx'), split_axis=0, concat_axis=0, t...  11.6 us
    all_to_all x1, starting transfers between devices, shards(): lax.all_to_all(slot_sent, ('slide', 'ctx'), split_axis=0, concat_axis=0,...  7.3 us
    all_to_all x1, starting transfers between devices, shards(): lax.all_to_all(outgoing, ('slide', 'ctx'), split_axis=0, concat_axis=0, t...  5.83 us
    slice x2, local copies, waits for them, and re-layouts, shards(): keys_part = key_rows[:, :model_width].reshape(row_count, HEADS, HEAD_DIM)  4.72 us
    dot_general x1, matrix products, shards(): jnp.dot(lnorm, key_weight, preferred_element_type=jnp.float32)  3.18 us
  transfers between devices with their start and end apart: 3, of which 2 were waited for; matrix products, arithmetic and copies ran while one was open for 5% of the time, Pallas kernels for 41%

profile of v1, /device:TPU:0, one launch (start us, length us, event | category | flops | bytes accessed | tf_op | source)
XLA Modules:
  0.0 144.2 jit_solution(8993583919128175307)
XLA Ops:
  6.5 0.0 copy-start
  6.5 0.8 fusion.26
  7.3 0.2 convert_reduce_fusion
  7.5 0.1 select_reduce_fusion
  7.6 0.1 sub.30
  7.7 0.6 compare_select_fusion
  8.3 7.3 %all-to-all-start = ((s32[32,6,1]{1,2,0:T(1,128)}), s32[32,6,1]{1,2,0:T(1,128)S(1)}, u32[]{:S(2)}, u32[]{:S(2)}) async-start(s32[32,6,1]{1,2,0:T(1,128)} %bitcast.1), calls=%async_computation | async-start | bytes 32768 | tf_op jit(solution)/shard_map/all_to_all | solution.py:156
  15.6 1.3 reshape.72.scale
  16.9 59.7 %encode.1 = bf16[32,768]{1,0:T(8,128)(2,1)} custom-call(bf16[32,256,384]{2,1,0:T(8,128)(2,1)} %bitcast.30, bf16[1536,768]{1,0:T(8,128)(2,1)} %down.1, bf16[49,768]{1,0:T(8,128)(2,1)} %taps.1, bf16[768,3072]{1,0:T(8,128)(2,1)} %win.1, bf16[3072,768]{1,0:T(8,128)(2,1)} %wout.1, f32[1,768]{1,0:T(1,128)} %reshape.72.scale, bf16[128,64]{1,0:T(8,128)(2,1)} %constant.63.clone.fwd, ...), custom_call_target="tpu_custom_call" | custom-call | tf_op jit(solution)/shard_map/encode/pallas_call | solution.py:106
  76.6 1.1 convolution_convert_fusion.1
  77.8 0.8 all_to_all.13
  78.6 0.0 all-to-all-done
  78.6 5.8 %all-to-all-start.1 = ((bf16[32,6,768]{2,1,0:T(8,128)(2,1)}), bf16[32,6,768]{2,1,0:T(8,128)(2,1)S(1)}, u32[]{:S(2)}, u32[]{:S(2)}) async-start(bf16[32,6,768]{2,1,0:T(8,128)(2,1)} %all_to_all.13), calls=%async_computation.1 | async-start | bytes 786432 | tf_op jit(solution)/shard_map/all_to_all | solution.py:155
  84.5 0.0 copy-start.2
  84.5 0.2 all-gather.2.cloned.1.call-start
  84.7 0.5 broadcast.83
  85.2 0.7 reduce.3
  85.9 0.1 eq.50
  86.0 11.6 %all-to-all-done.1 = bf16[32,6,768]{2,1,0:T(8,128)(2,1)S(1)} async-done(((bf16[32,6,768]{2,1,0:T(8,128)(2,1)}), bf16[32,6,768]{2,1,0:T(8,128)(2,1)S(1)}, u32[]{:S(2)}, u32[]{:S(2)}) %all-to-all-start.1) | async-done | bytes 294944 | tf_op jit(solution)/shard_map/all_to_all | solution.py:155
  97.6 0.1 all_to_all.15
  97.7 0.3 fusion.32
  98.1 0.2 multiply_reduce_fusion
  98.3 3.2 %convolution_convert_fusion = bf16[192,1536]{1,0:T(8,128)(2,1)} fusion(bf16[1,768,2304]{2,1,0:T(8,128)(2,1)} %param.21, f32[192,768]{1,0:T(8,128)S(1)} %get-tuple-element.10, f32[192]{0:T(256)S(1)} %add_rsqrt_fusion, f32[192]{0:T(256)S(1)} %broadcast_multiply_fusion), kind=kOutput, calls=%fused_computation.7 | convolution fusion | flops 453722112 | bytes 3540480 | tf_op jit(solution)/shard_map/dot_general | solution.py:170
  101.5 0.0 all-gather.2.cloned.1.call-update
  101.5 0.0 copy-done.2
  101.5 0.6 dynamic_slice.3
  102.1 0.7 add_compare_fusion
  102.8 0.7 iota_compare_fusion.5
  103.4 1.7 %convolution_convert_fusion.2 = bf16[192,768]{1,0:T(8,128)(2,1)S(1)} fusion(bf16[1,768,2304]{2,1,0:T(8,128)(2,1)} %param.21, f32[192,768]{1,0:T(8,128)S(1)} %get-tuple-element.10, f32[192]{0:T(256)S(1)} %add_rsqrt_fusion, f32[192]{0:T(256)S(1)} %broadcast_multiply_fusion), kind=kOutput, calls=%fused_computation.14 | convolution fusion | flops 227082240 | bytes 2065920 | tf_op jit(solution)/shard_map/dot_general | solution.py:168
  105.2 0.2 copy.27
  105.3 18.4 %all-gather.2.cloned.1.call-done = bf16[768,1536]{1,0:T(8,128)(2,1)} async-done(((bf16[192,1536]{1,0:T(8,128)(2,1)}), bf16[768,1536]{1,0:T(8,128)(2,1)}) %all-gather.2.cloned.1.call-update) | async-done | bytes 2359312 | tf_op jit(solution)/shard_map/all_gather | solution.py:171
  123.8 3.2 %fusion.31 = (bf16[768,768]{1,0:T(8,128)(2,1)}, bf16[768,768]{1,0:T(8,128)(2,1)}) fusion(bf16[768,1536]{1,0:T(8,128)(2,1)} %all-gather.2.cloned.1.call-done), kind=kLoop, calls=%fused_computation.48 | loop fusion | bytes 4718592 | tf_op jit(solution)/shard_map/slice | solution.py:174
  126.9 1.6 %copy.28 = bf16[768,768]{0,1:T(8,128)(2,1)S(1)} copy(bf16[768,768]{1,0:T(8,128)(2,1)} %get-tuple-element.5) | data formatting | bytes 2359296 | tf_op jit(solution)/shard_map/slice | solution.py:174
  128.5 2.4 %copy.29 = bf16[768,768]{0,1:T(8,128)(2,1)} copy(bf16[768,768]{1,0:T(8,128)(2,1)} %get-tuple-element.6) | data formatting | bytes 2359296 | tf_op jit(solution)/shard_map/slice | solution.py:175
  130.9 1.2 fusion
  132.1 0.0 copy-start.1
  132.2 2.0 %fusion.1 = f32[12,192]{1,0:T(8,128)S(1)} fusion(f32[12,192,768]{2,1,0:T(8,128)S(1)} %get-tuple-element.12, f32[12,192]{1,0:T(8,128)S(1)} %broadcast_maximum_fusion, pred[768]{0:T(1024)(128)(4,1)S(1)} %iota_compare_fusion.5), kind=kLoop, calls=%fused_computation.3 | loop fusion | flops 8845056 | bytes 7097088 | tf_op jit(solution)/shard_map/reduce_sum | solution.py:184
  134.1 0.0 copy-done.1
  134.1 2.1 %fusion.20 = bf16[192,12,64]{0,2,1:T(8,128)(2,1)S(1)} fusion(bf16[768,12,64]{0,2,1:T(8,128)(2,1)S(1)} %bitcast.33, f32[12,192,768]{2,1,0:T(8,128)S(1)} %get-tuple-element.12, f32[12,192]{1,0:T(8,128)S(1)} %broadcast_maximum_fusion, pred[768]{0:T(1024)(128)(4,1)S(1)} %iota_compare_fusion.5, f32[192,12]{0,1:T(8,128)S(1)} %bitcast.35), kind=kOutput, calls=%fused_computation.22 | convolution fusion | flops 235634688 | bytes 8571648 | tf_op jit(solution)/shard_map/hqk,khe->hqe/dot_general | solution.py:185
  136.2 0.0 copy-done
  136.2 1.1 fusion.13
  (5 shorter events, 0.0 us)
Async XLA Ops:
  6.5 129.7 %copy-start = (bf16[1,768,768]{2,1,0:T(8,128)(2,1)S(1)}, bf16[1,768,768]{2,1,0:T(8,128)(2,1)}, u32[]{:S(2)}) copy-start(bf16[1,768,768]{2,1,0:T(8,128)(2,1)} %param.22) | copy-start | bytes 3538948
  8.3 70.3 %all-to-all-start = ((s32[32,6,1]{1,2,0:T(1,128)}), s32[32,6,1]{1,2,0:T(1,128)S(1)}, u32[]{:S(2)}, u32[]{:S(2)}) async-start(s32[32,6,1]{1,2,0:T(1,128)} %bitcast.1), calls=%async_computation | async-start | bytes 32768 | tf_op jit(solution)/shard_map/all_to_all | solution.py:156
  78.6 19.0 %all-to-all-start.1 = ((bf16[32,6,768]{2,1,0:T(8,128)(2,1)}), bf16[32,6,768]{2,1,0:T(8,128)(2,1)S(1)}, u32[]{:S(2)}, u32[]{:S(2)}) async-start(bf16[32,6,768]{2,1,0:T(8,128)(2,1)} %all_to_all.13), calls=%async_computation.1 | async-start | bytes 786432 | tf_op jit(solution)/shard_map/all_to_all | solution.py:155
  84.5 17.1 %copy-start.2 = (s32[8]{0:T(128)S(1)}, s32[8]{0:T(128)}, u32[]{:S(2)}) copy-start(s32[8]{0:T(128)} %param.25) | copy-start | bytes 100
  84.5 39.3 %all-gather.2.cloned.1.call-start = ((), (), s32[]{:S(2)}) async-start(), calls=%async_computation.2 | async-start | bytes 2949120 | tf_op jit(solution)/shard_map/all_gather | solution.py:171
  132.1 2.0 %copy-start.1 = (bf16[768,768]{0,1:T(8,128)(2,1)S(1)}, bf16[768,768]{0,1:T(8,128)(2,1)}, u32[]{:S(2)}) copy-start(bf16[768,768]{0,1:T(8,128)(2,1)} %copy.29) | copy-start | bytes 3538948
Sparse Core Ops, SparseCore 0:
  101.6 22.0 all-gather.1

commit v2 on v1

v2 whole, which is shorter than its diff:
```python
import functools

import jax
import jax.numpy as jnp
import numpy as np
from jax import lax
from jax.experimental import pallas as pl
from jax.experimental.pallas import tpu as pltpu
from jax.sharding import PartitionSpec as P

HEADS = 12
HEAD_DIM = 64
SEQ_DEV = 192
META = 128
NORM_EPS = 1e-06
FAR_NEGATIVE = -1e30
F32=jnp.float32; BF=jnp.bfloat16
FREQ=64
C0,C1,C2=0.796875,0.03759765625,-0.000457763671875

def tables(side, ks):
    reach=ks//2; n=side+reach
    half=[(0,0)]+[(0,l) for l in range(1,n//2+1)]+[(k,l) for k in range(1,n//2+1) for l in range(n)]
    k=np.array([a for a,_ in half]); l=np.array([b for _,b in half])
    pos=np.arange(side*side); i,j=pos//side,pos%side
    th=2*np.pi*(np.outer(k,i)+np.outer(l,j))/n
    fwd=np.zeros((2*FREQ,side*side)); fwd[:len(half)]=np.cos(th); fwd[FREQ:FREQ+len(half)]=-np.sin(th)
    a=np.arange(ks*ks)//ks-reach; b=np.arange(ks*ks)%ks-reach
    ph=2*np.pi*(np.outer(k,a)+np.outer(l,b))/n
    s=np.where(np.arange(len(half))==0,1.0,2.0)[:,None]/(n*n)
    tap=np.zeros((2*FREQ,ks*ks)); tap[:len(half)]=s*np.cos(ph); tap[FREQ:FREQ+len(half)]=s*np.sin(ph)
    inv=fwd.T.copy()
    perm=np.zeros((4*side*side,4*side*side))
    for dy in range(2):
        for dx in range(2):
            for ii in range(side):
                for jj in range(side):
                    perm[(dy*2+dx)*side*side+ii*side+jj,(2*ii+dy)*2*side+2*jj+dx]=1
    hi=tap.astype(jnp.bfloat16).astype(np.float64)
    return fwd, inv, np.concatenate([hi,tap-hi]), perm

def rows_norm(x):
    c=x-jnp.mean(x,axis=-1,keepdims=True)
    return c*lax.rsqrt(jnp.mean(c*c,axis=-1,keepdims=True)+NORM_EPS)

def gelu_sums(h, tiles, rows):
    b=h.astype(BF)
    w=jnp.minimum(b*b, jnp.asarray(50.0,BF))
    p=jnp.asarray(C0,BF)+w*(jnp.asarray(C1,BF)+jnp.asarray(C2,BF)*w)
    e=b+b*jnp.tanh(b*p)
    e=e.reshape(tiles,rows//16,16,h.shape[1])
    parts=[e[:,i] for i in range(rows//16)]
    while len(parts)>1:
        parts=[a+c for a,c in zip(parts[::2],parts[1::2])]
    s=parts[0].astype(F32).reshape(tiles,2,8,h.shape[1])
    return (s[:,0]+s[:,1]).reshape(tiles*8,h.shape[1])

def meta_cols(slides, places, count, blocks):
    row=lax.broadcasted_iota(jnp.int32,(count,META),0)
    lane=lax.broadcasted_iota(jnp.int32,(count,META),1)
    cols=jnp.zeros((count,META),jnp.int32)
    for t in range(count):
        place=places[t]
        block=jnp.int32(0)
        for edge in range(1,blocks):
            block=block+(place>=edge*SEQ_DEV).astype(jnp.int32)
        vals=jnp.where(lane==0,slides[t],jnp.where(lane==1,block,place-block*SEQ_DEV))
        cols=jnp.where((row==t)&(lane<3),vals,cols)
    return cols.astype(F32).astype(BF)

def kernel(G, side, blocks, NC, steps, feat, down_h, taps, win_h, wout_h, scale, slides, places, fwd, inv, taptab, perm, out,
           patches, red, sn_a, sn_b, psum, pool, khat, down, win, wout, hbuf, sems):
    step=pl.program_id(0)
    S=side*side
    C=feat.shape[-1]; D=down.shape[1]; M=win.shape[1]; T=out.shape[0]
    cp_down=pltpu.make_async_copy(down_h,down,sems.at[0])
    cp_in=pltpu.make_async_copy(win_h,win,sems.at[1])
    cp_out=pltpu.make_async_copy(wout_h,wout,sems.at[2])

    def a1(t):
        xp=jnp.dot(perm[...],feat[t],preferred_element_type=F32)
        n=rows_norm(xp).astype(BF)
        for q in range(4):
            patches[t*S:(t+1)*S, q*C:(q+1)*C]=n[q*S:(q+1)*S]
    def a2(c, w):
        red[:,c*w:(c+1)*w]=jnp.dot(patches[...],down[:,c*w:(c+1)*w],preferred_element_type=F32).astype(BF)
    def a3(t):
        f=jnp.dot(fwd[...],red[t*S:(t+1)*S,:],preferred_element_type=F32)
        pool[pl.ds(step*G+t,1),:]=f[0:1]*(1.0/S)
        fr,fi=f[:FREQ],f[FREQ:]
        kr,ki=khat[:FREQ,:],khat[FREQ:,:]
        g=jnp.concatenate([fr*kr-fi*ki, fr*ki+fi*kr],axis=0).astype(BF)
        sp=jnp.dot(inv[...],g,preferred_element_type=F32)
        sn_a[t*S:(t+1)*S,:]=rows_norm(sp).astype(BF)
    def b1(c):
        hbuf[c%2]=jnp.dot(sn_b[...],win[:,c*NC:(c+1)*NC],preferred_element_type=F32).astype(hbuf.dtype)
    def b2(c):
        psum[pl.ds(pl.multiple_of((step-1)*G*8,G*8),G*8), c*NC:(c+1)*NC]=gelu_sums(hbuf[c%2],G,S).astype(BF)
    a_items=[(lambda t=t:a1(t)) for t in range(G)]+[(lambda c=c:a2(c,256)) for c in range(D//256)]+[(lambda t=t:a3(t)) for t in range(G)]
    b_items=[]
    for c in range(M//NC+1):
        def item(c=c):
            if c<M//NC: b1(c)
            if c>0: b2(c-1)
        b_items.append(item)
    def keep():
        sn_b[...]=sn_a[...]

    @pl.when(step==0)
    def _():
        cp_down.start(); cp_in.start(); cp_out.start()
        t2=jnp.dot(taptab[...],taps[...],preferred_element_type=F32)
        khat[...]=t2[:2*FREQ]+t2[2*FREQ:]
        for t in range(G): a1(t)
        cp_down.wait()
        for f in a_items[G:]: f()
        cp_in.wait()
        keep()
    @pl.when((step>0)&(step<steps))
    def _():
        na,nb=len(a_items),len(b_items)
        done=0
        for i,f in enumerate(b_items):
            f()
            upto=(i+1)*na//nb
            for g in a_items[done:upto]: g()
            done=upto
        keep()
    @pl.when(step==steps)
    def _():
        for f in b_items: f()
        cp_out.wait()
        z=jnp.dot(psum[...],wout[...],preferred_element_type=F32)
        z=z.reshape(z.shape[0]//8,8,D).sum(axis=1)*(0.5/S)
        out[:,:D]=rows_norm(pool[...]+scale[...].reshape(1,D)*z).astype(BF)
        out[:,D:]=meta_cols(slides,places,T,blocks)

def encode(feature_maps, down, taps, win, wout, scale, tile_slide, tile_pos, G=8, NC=256, hb=BF):
    T,H,W,C=feature_maps.shape
    side=H//2; S=side*side; D=down.shape[1]; M=win.shape[1]; ks=int(round(taps.shape[0]**.5))
    fwd,inv,tt,perm=tables(side,ks)
    blocks=lax.axis_size("ctx")
    steps=T//G
    full=lambda a: pl.BlockSpec(a.shape,lambda s:(0,)*a.ndim,pipeline_mode=pl.Buffered(1))
    hbm=pl.BlockSpec(memory_space=pl.ANY); smem=pl.BlockSpec(memory_space=pltpu.SMEM)
    tabs=[jnp.asarray(a,BF) for a in (fwd,inv,tt,perm)]
    r=pl.pallas_call(
        functools.partial(kernel,G,side,blocks,NC,steps),
        grid=(steps+1,),
        in_specs=[pl.BlockSpec((G,H*W,C),lambda s:(jnp.minimum(s,steps-1),0,0)),hbm,full(taps),hbm,hbm,full(scale),smem,smem]+[full(a) for a in tabs],
        out_specs=pl.BlockSpec((T,D+META),lambda s:(0,0)),
        out_shape=jax.ShapeDtypeStruct((T,D+META),BF),
        scratch_shapes=[pltpu.VMEM((G*S,4*C),BF),pltpu.VMEM((G*S,D),BF),pltpu.VMEM((G*S,D),BF),pltpu.VMEM((G*S,D),BF),
                        pltpu.VMEM((T*8,M),BF),pltpu.VMEM((T,D),F32),pltpu.VMEM((2*FREQ,D),F32),
                        pltpu.VMEM(down.shape,BF),pltpu.VMEM(win.shape,BF),pltpu.VMEM(wout.shape,BF),
                        pltpu.VMEM((2,G*S,NC),hb),pltpu.SemaphoreType.DMA((3,))],
        compiler_params=pltpu.CompilerParams(vmem_limit_bytes=60*1024*1024, dimension_semantics=("arbitrary",)),
        name="encode",
    )(feature_maps.reshape(T,H*W,C),down,taps,win,wout,scale,tile_slide,tile_pos,*tabs)
    return r


def gather_rows(rows, count):
    span_left = count
    while span_left > 1:
        span = 4 if span_left >= 4 else 2
        unit = span_left // span
        parts = [rows]
        for mask in range(1, span):
            pairs = [(dev, dev ^ (mask * unit)) for dev in range(count)]
            parts.append(lax.ppermute(rows, ("slide", "ctx"), pairs))
        span_left = unit
        if span_left > 1:
            rows = jnp.concatenate(parts, axis=0)
    return parts


def attend_kernel(part_count, chunk, *refs):
    parts = refs[:part_count]
    qkv, wout, lens, out, keyvals, bias, attended = refs[part_count:]
    D = wout.shape[0]
    rows_dev = out.shape[0]
    part_rows = parts[0].shape[0]
    my_slide = lax.axis_index("slide")
    my_ctx = lax.axis_index("ctx")
    length = lens[my_slide]
    slide_f = my_slide.astype(F32)
    ctx_f = my_ctx.astype(F32)
    pick_lane = (
        lax.broadcasted_iota(jnp.int32, (8, META), 0) == lax.broadcasted_iota(jnp.int32, (8, META), 1)
    ).astype(BF)
    slot = lax.broadcasted_iota(jnp.int32, (rows_dev, 1), 0).astype(F32)
    stream = jnp.zeros((rows_dev, D), F32)
    for index, part in enumerate(parts):
        ids = lax.dot_general(
            pick_lane, part[:, D:], (((1,), (1,)), ((), ())), preferred_element_type=F32
        )
        here = ids[0:1] == slide_f
        place = ids[1:2] * float(rows_dev) + ids[2:3]
        included = here & (place < length.astype(F32))
        bias[:, index * part_rows : (index + 1) * part_rows] = jnp.where(included, 0.0, FAR_NEGATIVE)
        target = jnp.where(here & (ids[1:2] == ctx_f), ids[2:3], -1.0)
        picking = (slot == target).astype(BF)
        stream = stream + jnp.dot(picking, part[:, :D], preferred_element_type=F32)
        for start in range(0, part_rows, chunk):
            lnorm = rows_norm(part[start : start + chunk, :D].astype(F32)).astype(BF)
            keyvals[index * part_rows + start : index * part_rows + start + chunk, :] = jnp.dot(
                lnorm, qkv[:, D:], preferred_element_type=F32
            ).astype(BF)
    lnorm = rows_norm(stream).astype(BF)
    queries = jnp.dot(lnorm, qkv[:, :D], preferred_element_type=F32).astype(BF)
    lane = lax.broadcasted_iota(jnp.int32, (1, 2 * HEAD_DIM), 1)
    low = lane < HEAD_DIM
    scale = jnp.asarray(HEAD_DIM**-0.5, BF)
    for pair in range(HEADS // 2):
        cols = slice(pair * 2 * HEAD_DIM, (pair + 1) * 2 * HEAD_DIM)
        vcols = slice(D + pair * 2 * HEAD_DIM, D + (pair + 1) * 2 * HEAD_DIM)
        both = queries[:, cols] * scale
        zero = jnp.zeros_like(both)
        stacked = jnp.concatenate([jnp.where(low, both, zero), jnp.where(low, zero, both)], axis=0)
        scores = lax.dot_general(
            stacked, keyvals[:, cols], (((1,), (1,)), ((), ())), preferred_element_type=F32
        )
        scores = scores + bias[...]
        weights = jnp.exp(scores - jnp.max(scores, axis=-1, keepdims=True))
        denom = jnp.sum(weights, axis=-1, keepdims=True)
        mixed = jnp.dot(weights.astype(BF), keyvals[:, vcols], preferred_element_type=F32) / denom
        attended[:, cols] = jnp.where(low, mixed[:rows_dev], mixed[rows_dev:]).astype(BF)
    stream = stream + jnp.dot(attended[...], wout[...], preferred_element_type=F32)
    valid = (slot + ctx_f * float(rows_dev)) < length.astype(F32)
    out[...] = jnp.where(valid, stream, 0.0).astype(BF)


def attend(parts, qkv, wout, lens):
    D = wout.shape[0]
    total = len(parts) * parts[0].shape[0]
    chunk = min(256, parts[0].shape[0])
    vmem = pl.BlockSpec(memory_space=pltpu.VMEM)
    return pl.pallas_call(
        functools.partial(attend_kernel, len(parts), chunk),
        in_specs=[vmem] * (len(parts) + 2) + [pl.BlockSpec(memory_space=pltpu.SMEM)],
        out_specs=vmem,
        out_shape=jax.ShapeDtypeStruct((SEQ_DEV, D), BF),
        scratch_shapes=[
            pltpu.VMEM((total, 2 * D), BF),
            pltpu.VMEM((1, total), F32),
            pltpu.VMEM((SEQ_DEV, D), BF),
        ],
        compiler_params=pltpu.CompilerParams(vmem_limit_bytes=56 * 1024 * 1024),
        name="attend",
    )(*parts, qkv, wout, lens)


def shards(
    feature_maps,
    down_weight,
    conv_taps,
    mlp_in,
    mlp_out,
    layer_scale,
    qkv_weight,
    out_weight,
    tile_slide,
    tile_pos,
    slide_len,
):
    device_count = lax.axis_size("slide") * lax.axis_size("ctx")
    rows = encode(
        feature_maps, down_weight, conv_taps, mlp_in, mlp_out, layer_scale, tile_slide, tile_pos
    )
    parts = gather_rows(rows, device_count)
    return attend(parts, qkv_weight[0], out_weight[0], slide_len)


def solution(mesh):
    return jax.shard_map(
        shards,
        mesh=mesh,
        in_specs=(
            P(("slide", "ctx"), None, None, None),
            P(),
            P(),
            P(),
            P(),
            P(),
            P(),
            P(),
            P(("slide", "ctx")),
            P(("slide", "ctx")),
            P(),
        ),
        out_specs=P(("slide", "ctx"), None),
        check_vma=False,
    )
```

time: 145 us -> 71.5 us (0.49)
  Pallas kernels: 59.7 us -> 43.1 us
  waiting for transfers between devices: 30.1 us -> 16 us
  between operations: 13.6 us -> 0.05 us
  matrix products: 10.8 us -> 0 us
  local copies, waits for them, and re-layouts: 10.8 us -> 1.96 us
  other arithmetic: 5.87 us -> 0.84 us
  starting transfers between devices: 13.4 us -> 9.29 us
    all_gather x1 -> x0, waiting for transfers between devices: 18.4 us -> none  [shards(): key_rows = lax.all_gather(local_kv, 'ctx', axis=0, tiled=True)]
    pallas_call x1 -> x2, Pallas kernels: 59.7 us -> 43.1 us  [the longest x1 32 us: encode(): pl.pallas_call(functools.partial(kernel, G, side, blocks, NC, steps), gri...]
    ppermute x0 -> x7, waiting for transfers between devices: none -> 16 us  [gather_rows(): parts.append(lax.ppermute(rows, ('slide', 'ctx'), pairs))]
    all_to_all x2 -> x0, starting transfers between devices: 13.1 us -> none  [the longest x1 7.3 us: shards(): lax.all_to_all(slot_sent, ('slide', 'ctx'), split_axis=0, concat_axis=0,...]
    all_to_all x2 -> x0, waiting for transfers between devices: 11.6 us -> none  [the longest x1 11.6 us: shards(): lax.all_to_all(outgoing, ('slide', 'ctx'), split_axis=0, concat_axis=0, t...]
    dot_general x7 -> x0, matrix products: 10.8 us -> none  [the longest x1 3.18 us: shards(): jnp.dot(lnorm, key_weight, preferred_element_type=jnp.float32)]
    ppermute x0 -> x7, starting transfers between devices: none -> 9.29 us  [gather_rows(): parts.append(lax.ppermute(rows, ('slide', 'ctx'), pairs))]
    slice x3 -> x0, local copies, waits for them, and re-layouts: 7.09 us -> none  [the longest x2 4.72 us: shards(): keys_part = key_rows[:, :model_width].reshape(row_count, HEADS, HEAD_DIM)]
  transfers between devices with their start and end apart: 3 -> 7, of which waited for: 2 -> 6; matrix products, arithmetic and copies ran while one was open for 5% -> 1% of each run, Pallas kernels for 41% -> 0%
where the time goes in v2:
time: 71.5 us; the launch traced here: 71.2 us
  Pallas kernels  43.1 us (60%)
  waiting for transfers between devices  16 us (22%)
  starting transfers between devices  9.29 us (13%)
  local copies, waits for them, and re-layouts  1.96 us (3%)
  other arithmetic  0.84 us (1%)
    pallas_call x1, Pallas kernels, encode(): pl.pallas_call(functools.partial(kernel, G, side, blocks, NC, steps), gri...  32 us
    ppermute x7, waiting for transfers between devices, gather_rows(): parts.append(lax.ppermute(rows, ('slide', 'ctx'), pairs))  16 us
    pallas_call x1, Pallas kernels, attend(): pl.pallas_call(functools.partial(attend_kernel, len(parts), chunk), in_sp...  11.1 us
    ppermute x7, starting transfers between devices, gather_rows(): parts.append(lax.ppermute(rows, ('slide', 'ctx'), pairs))  9.29 us
    unnamed x10, local copies, waits for them, and re-layouts  1.93 us
  transfers between devices with their start and end apart: 7, of which 6 were waited for; matrix products, arithmetic and copies ran while one was open for 1% of the time, Pallas kernels for 0%

profile of v2, /device:TPU:0, one launch (start us, length us, event | category | flops | bytes accessed | tf_op | source)
XLA Modules:
  0.0 71.2 jit_solution(17868136618840183671)
XLA Ops:
  0.0 32.0 %encode.1 = bf16[32,896]{1,0:T(8,128)(2,1)} custom-call(bf16[32,256,384]{2,1,0:T(8,128)(2,1)} %bitcast.3, bf16[1536,768]{1,0:T(8,128)(2,1)} %down_h.1, bf16[49,768]{1,0:T(8,128)(2,1)} %taps.1, bf16[768,3072]{1,0:T(8,128)(2,1)} %win_h.1, bf16[3072,768]{1,0:T(8,128)(2,1)} %wout_h.1, f32[768]{0:T(1024)} %scale.1, s32[32]{0:T(128)} %slides.1, s32[32]{0:T(128)} %places.1, ...), custom_call_target="tpu_custom_call" | custom-call | tf_op jit(solution)/shard_map/encode/pallas_call | solution.py:147
  32.0 3.1 %collective-permute-start = (bf16[32,896]{1,0:T(8,128)(2,1)}, bf16[32,896]{1,0:T(8,128)(2,1)S(1)}, u32[]{:S(2)}, u32[]{:S(2)}) collective-permute-start(bf16[32,896]{1,0:T(8,128)(2,1)} %encode.1), channel_id=1, source_target_pairs={{0,8},{1,9},{2,10},{3,11},{4,12},{5,13},{6,14},{7,15},{8,0},{9,1},... | collective-permute-start | bytes 172040 | tf_op jit(solution)/shard_map/ppermute | solution.py:171
  35.1 2.6 %collective-permute-start.1 = (bf16[32,896]{1,0:T(8,128)(2,1)}, bf16[32,896]{1,0:T(8,128)(2,1)S(1)}, u32[]{:S(2)}, u32[]{:S(2)}) collective-permute-start(bf16[32,896]{1,0:T(8,128)(2,1)} %encode.1), channel_id=1, source_target_pairs={{0,16},{1,17},{2,18},{3,19},{4,20},{5,21},{6,22},{7,23},{8,24},{9,... | collective-permute-start | bytes 172040 | tf_op jit(solution)/shard_map/ppermute | solution.py:171
  37.7 0.0 collective-permute-start.2
  37.7 0.9 %constant_dynamic-update-slice_fusion.6 = bf16[512,896]{1,0:T(8,128)(2,1)S(1)} fusion(bf16[32,896]{1,0:T(8,128)(2,1)} %encode.1), kind=kLoop, calls=%fused_computation.7 | loop fusion | bytes 114688
  38.6 0.0 collective-permute-done
  38.6 2.9 %collective-permute-done.1 = bf16[32,896]{1,0:T(8,128)(2,1)S(1)} collective-permute-done((bf16[32,896]{1,0:T(8,128)(2,1)}, bf16[32,896]{1,0:T(8,128)(2,1)S(1)}, u32[]{:S(2)}, u32[]{:S(2)}) %collective-permute-start.1) | collective-permute-done | bytes 57376 | tf_op jit(solution)/shard_map/ppermute | solution.py:171
  41.5 2.4 %collective-permute-done.2 = bf16[32,896]{1,0:T(8,128)(2,1)S(1)} collective-permute-done((bf16[32,896]{1,0:T(8,128)(2,1)}, bf16[32,896]{1,0:T(8,128)(2,1)S(1)}, u32[]{:S(2)}, u32[]{:S(2)}) %collective-permute-start.2) | collective-permute-done | bytes 57376 | tf_op jit(solution)/shard_map/ppermute | solution.py:171
  43.9 0.8 %pad_maximum_fusion = bf16[128,896]{1,0:T(8,128)(2,1)S(1)} fusion(bf16[32,896]{1,0:T(8,128)(2,1)S(1)} %collective-permute-done.2, bf16[32,896]{1,0:T(8,128)(2,1)S(1)} %collective-permute-done.1, bf16[32,896]{1,0:T(8,128)(2,1)S(1)} %collective-permute-done, bf16[32,896]{1,0:T(8,128)(2,1)} %encode.1), kind=kLoop, calls=%fused_computation | loop fusion | flops 917504 | bytes 458752 | tf_op jit(solution)/shard_map/concatenate | solution.py:174
  44.7 1.6 %collective-permute-start.3 = (bf16[128,896]{1,0:T(8,128)(2,1)S(1)}, bf16[128,896]{1,0:T(8,128)(2,1)S(1)}, u32[]{:S(2)}, u32[]{:S(2)}) collective-permute-start(bf16[128,896]{1,0:T(8,128)(2,1)S(1)} %pad_maximum_fusion), channel_id=1, source_target_pairs={{0,2},{1,3},{2,0},{3,1},{4,6},{5,7},{6,4},{7,5},{8,10},{9,11},{10,... | collective-permute-start | bytes 688136 | tf_op jit(solution)/shard_map/ppermute | solution.py:171
  46.3 1.5 %collective-permute-start.4 = (bf16[128,896]{1,0:T(8,128)(2,1)S(1)}, bf16[128,896]{1,0:T(8,128)(2,1)S(1)}, u32[]{:S(2)}, u32[]{:S(2)}) collective-permute-start(bf16[128,896]{1,0:T(8,128)(2,1)S(1)} %pad_maximum_fusion), channel_id=1, source_target_pairs={{0,4},{1,5},{2,6},{3,7},{4,0},{5,1},{6,2},{7,3},{8,12},{9,13},{10,... | collective-permute-start | bytes 688136 | tf_op jit(solution)/shard_map/ppermute | solution.py:171
  47.8 0.5 collective-permute-start.5
  48.3 4.7 %collective-permute-done.3 = bf16[128,896]{1,0:T(8,128)(2,1)S(1)} collective-permute-done((bf16[128,896]{1,0:T(8,128)(2,1)S(1)}, bf16[128,896]{1,0:T(8,128)(2,1)S(1)}, u32[]{:S(2)}, u32[]{:S(2)}) %collective-permute-start.3) | collective-permute-done | bytes 229408 | tf_op jit(solution)/shard_map/ppermute | solution.py:171
  53.0 1.2 %collective-permute-done.4 = bf16[128,896]{1,0:T(8,128)(2,1)S(1)} collective-permute-done((bf16[128,896]{1,0:T(8,128)(2,1)S(1)}, bf16[128,896]{1,0:T(8,128)(2,1)S(1)}, u32[]{:S(2)}, u32[]{:S(2)}) %collective-permute-start.4) | collective-permute-done | bytes 229408 | tf_op jit(solution)/shard_map/ppermute | solution.py:171
  54.3 2.4 %collective-permute-done.5 = bf16[128,896]{1,0:T(8,128)(2,1)S(1)} collective-permute-done((bf16[128,896]{1,0:T(8,128)(2,1)S(1)}, bf16[128,896]{1,0:T(8,128)(2,1)S(1)}, u32[]{:S(2)}, u32[]{:S(2)}) %collective-permute-start.5) | collective-permute-done | bytes 229408 | tf_op jit(solution)/shard_map/ppermute | solution.py:171
  56.7 0.0 copy-start
  56.7 0.1 collective-permute-start.6
  56.8 2.5 %collective-permute-done.6.refs_1_ = bf16[512,896]{1,0:T(8,128)(2,1)S(1)} collective-permute-done((bf16[512,896]{1,0:T(8,128)(2,1)S(1)}, bf16[512,896]{1,0:T(8,128)(2,1)S(1)}, u32[]{:S(2)}, u32[]{:S(2)}) %collective-permute-start.6) | collective-permute-done | bytes 917536 | tf_op jit(solution)/shard_map/ppermute | solution.py:171
  59.2 0.0 copy-start.1
  59.2 0.0 copy-done
  59.2 1.0 %copy-done.1 = bf16[512,896]{1,0:T(8,128)(2,1)} copy-done((bf16[512,896]{1,0:T(8,128)(2,1)}, bf16[512,896]{1,0:T(8,128)(2,1)S(1)}, u32[]{:S(2)}) %copy-start.1) | copy-done | bytes 917528
  60.2 11.1 %attend.1 = bf16[192,768]{1,0:T(8,128)(2,1)} custom-call(bf16[512,896]{1,0:T(8,128)(2,1)} %copy-done, bf16[512,896]{1,0:T(8,128)(2,1)} %copy-done.1, bf16[768,2304]{1,0:T(8,128)(2,1)} %bitcast.4, bf16[768,768]{1,0:T(8,128)(2,1)} %bitcast.5, s32[8]{0:T(128)} %refs_4_.1), custom_call_target="tpu_custom_call" | custom-call | tf_op jit(solution)/shard_map/attend/pallas_call | solution.py:239
  (6 shorter events, 0.1 us)
Async XLA Ops:
  32.0 6.6 %collective-permute-start = (bf16[32,896]{1,0:T(8,128)(2,1)}, bf16[32,896]{1,0:T(8,128)(2,1)S(1)}, u32[]{:S(2)}, u32[]{:S(2)}) collective-permute-start(bf16[32,896]{1,0:T(8,128)(2,1)} %encode.1), channel_id=1, source_target_pairs={{0,8},{1,9},{2,10},{3,11},{4,12},{5,13},{6,14},{7,15},{8,0},{9,1},... | collective-permute-start | bytes 172040 | tf_op jit(solution)/shard_map/ppermute | solution.py:171
  35.1 6.4 %collective-permute-start.1 = (bf16[32,896]{1,0:T(8,128)(2,1)}, bf16[32,896]{1,0:T(8,128)(2,1)S(1)}, u32[]{:S(2)}, u32[]{:S(2)}) collective-permute-start(bf16[32,896]{1,0:T(8,128)(2,1)} %encode.1), channel_id=1, source_target_pairs={{0,16},{1,17},{2,18},{3,19},{4,20},{5,21},{6,22},{7,23},{8,24},{9,... | collective-permute-start | bytes 172040 | tf_op jit(solution)/shard_map/ppermute | solution.py:171
  37.7 6.2 %collective-permute-start.2 = (bf16[32,896]{1,0:T(8,128)(2,1)}, bf16[32,896]{1,0:T(8,128)(2,1)S(1)}, u32[]{:S(2)}, u32[]{:S(2)}) collective-permute-start(bf16[32,896]{1,0:T(8,128)(2,1)} %encode.1), channel_id=1, source_target_pairs={{0,24},{1,25},{2,26},{3,27},{4,28},{5,29},{6,30},{7,31},{8,16},{9,... | collective-permute-start | bytes 172040 | tf_op jit(solution)/shard_map/ppermute | solution.py:171
  44.7 8.3 %collective-permute-start.3 = (bf16[128,896]{1,0:T(8,128)(2,1)S(1)}, bf16[128,896]{1,0:T(8,128)(2,1)S(1)}, u32[]{:S(2)}, u32[]{:S(2)}) collective-permute-start(bf16[128,896]{1,0:T(8,128)(2,1)S(1)} %pad_maximum_fusion), channel_id=1, source_target_pairs={{0,2},{1,3},{2,0},{3,1},{4,6},{5,7},{6,4},{7,5},{8,10},{9,11},{10,... | collective-permute-start | bytes 688136 | tf_op jit(solution)/shard_map/ppermute | solution.py:171
  46.3 7.9 %collective-permute-start.4 = (bf16[128,896]{1,0:T(8,128)(2,1)S(1)}, bf16[128,896]{1,0:T(8,128)(2,1)S(1)}, u32[]{:S(2)}, u32[]{:S(2)}) collective-permute-start(bf16[128,896]{1,0:T(8,128)(2,1)S(1)} %pad_maximum_fusion), channel_id=1, source_target_pairs={{0,4},{1,5},{2,6},{3,7},{4,0},{5,1},{6,2},{7,3},{8,12},{9,13},{10,... | collective-permute-start | bytes 688136 | tf_op jit(solution)/shard_map/ppermute | solution.py:171
  47.8 8.8 %collective-permute-start.5 = (bf16[128,896]{1,0:T(8,128)(2,1)S(1)}, bf16[128,896]{1,0:T(8,128)(2,1)S(1)}, u32[]{:S(2)}, u32[]{:S(2)}) collective-permute-start(bf16[128,896]{1,0:T(8,128)(2,1)S(1)} %pad_maximum_fusion), channel_id=1, source_target_pairs={{0,6},{1,7},{2,4},{3,5},{4,2},{5,3},{6,0},{7,1},{8,14},{9,15},{10,... | collective-permute-start | bytes 688136 | tf_op jit(solution)/shard_map/ppermute | solution.py:171
  56.7 2.6 %copy-start = (bf16[512,896]{1,0:T(8,128)(2,1)}, bf16[512,896]{1,0:T(8,128)(2,1)S(1)}, u32[]{:S(2)}) copy-start(bf16[512,896]{1,0:T(8,128)(2,1)S(1)} %constant_dynamic-update-slice_fusion.refs_0_) | copy-start | bytes 2752516
  56.7 2.5 %collective-permute-start.6 = (bf16[512,896]{1,0:T(8,128)(2,1)S(1)}, bf16[512,896]{1,0:T(8,128)(2,1)S(1)}, u32[]{:S(2)}, u32[]{:S(2)}) collective-permute-start(bf16[512,896]{1,0:T(8,128)(2,1)S(1)} %constant_dynamic-update-slice_fusion.refs_0_), channel_id=1, source_target_pairs={{0,1},{1,0},{2,3},{3,2},{4,5},{5,4},{6,7},{7,6},{8,9},{9,8},{10,11... | collective-permute-start | bytes 2752520 | tf_op jit(solution)/shard_map/ppermute | solution.py:171
  59.2 1.0 %copy-start.1 = (bf16[512,896]{1,0:T(8,128)(2,1)}, bf16[512,896]{1,0:T(8,128)(2,1)S(1)}, u32[]{:S(2)}) copy-start(bf16[512,896]{1,0:T(8,128)(2,1)S(1)} %collective-permute-done.6.refs_1_) | copy-start | bytes 2752516

commit v3 on v2

v3 whole, which is shorter than its diff:
```python
import functools

import jax
import jax.numpy as jnp
import numpy as np
from jax import lax
from jax.experimental import pallas as pl
from jax.experimental.pallas import tpu as pltpu
from jax.sharding import PartitionSpec as P

HEADS = 12
HEAD_DIM = 64
SEQ_DEV = 192
META = 128
NORM_EPS = 1e-06
FAR_NEGATIVE = -1e30
F32=jnp.float32; BF=jnp.bfloat16
FREQ=64
FT,IT=4,2
VM=58
C0,C1,C2=0.796875,0.03759765625,-0.000457763671875

def tables(side, ks):
    reach=ks//2; n=side+reach
    half=[(0,0)]+[(0,l) for l in range(1,n//2+1)]+[(k,l) for k in range(1,n//2+1) for l in range(n)]
    k=np.array([a for a,_ in half]); l=np.array([b for _,b in half])
    pos=np.arange(side*side); i,j=pos//side,pos%side
    th=2*np.pi*(np.outer(k,i)+np.outer(l,j))/n
    fwd=np.zeros((2*FREQ,side*side)); fwd[:len(half)]=np.cos(th); fwd[FREQ:FREQ+len(half)]=-np.sin(th)
    a=np.arange(ks*ks)//ks-reach; b=np.arange(ks*ks)%ks-reach
    ph=2*np.pi*(np.outer(k,a)+np.outer(l,b))/n
    s=np.where(np.arange(len(half))==0,1.0,2.0)[:,None]/(n*n)
    tap=np.zeros((2*FREQ,ks*ks)); tap[:len(half)]=s*np.cos(ph); tap[FREQ:FREQ+len(half)]=s*np.sin(ph)
    inv=fwd.T.copy()
    hi=tap.astype(jnp.bfloat16).astype(np.float64)
    return fwd, inv, np.concatenate([hi,tap-hi])

def rows_norm(x):
    c=x-jnp.mean(x,axis=-1,keepdims=True)
    return c*lax.rsqrt(jnp.mean(c*c,axis=-1,keepdims=True)+NORM_EPS)

def gelu_sums(h, tiles, rows):
    b=h.astype(BF)
    w=jnp.minimum(b*b, jnp.asarray(50.0,BF))
    p=jnp.asarray(C0,BF)+w*(jnp.asarray(C1,BF)+jnp.asarray(C2,BF)*w)
    e=b+b*jnp.tanh(b*p)
    e=e.reshape(tiles,rows//16,16,h.shape[1])
    parts=[e[:,i] for i in range(rows//16)]
    while len(parts)>1:
        parts=[a+c for a,c in zip(parts[::2],parts[1::2])]
    s=parts[0].astype(F32).reshape(tiles,2,8,h.shape[1])
    return (s[:,0]+s[:,1]).reshape(tiles*8,h.shape[1])

def meta_cols(slides, places, count, blocks):
    row=lax.broadcasted_iota(jnp.int32,(count,META),0)
    lane=lax.broadcasted_iota(jnp.int32,(count,META),1)
    cols=jnp.zeros((count,META),jnp.int32)
    for t in range(count):
        place=places[t]
        block=jnp.int32(0)
        for edge in range(1,blocks):
            block=block+(place>=edge*SEQ_DEV).astype(jnp.int32)
        vals=jnp.where(lane==0,slides[t],jnp.where(lane==1,block,place-block*SEQ_DEV))
        cols=jnp.where((row==t)&(lane<3),vals,cols)
    return cols.astype(F32).astype(BF)

def kernel(G, side, blocks, NC, steps, feat, down_h, win_h, wout_h, taps_h, fwd_h, inv_h, taptab_h, scale, slides, places, out,
           patches, red, sn_a, sn_b, psum, pool, khat, hbuf, down, win, wout, taps, fwd, inv, taptab, normed, sems):
    step=pl.program_id(0)
    S=side*side
    C=feat.shape[-1]; D=down.shape[1]; M=win.shape[1]; T=out.shape[0]
    def copy(src,dst,index):
        return pltpu.make_async_copy(src,dst,sems.at[index])
    cp_down=copy(down_h,down,0)
    cp_in=copy(win_h,win,1)
    cp_out=copy(wout_h,wout,2)
    cp_small=[copy(a,b,3+i) for i,(a,b) in enumerate([(taps_h,taps),(taptab_h,taptab),(fwd_h,fwd),(inv_h,inv)])]

    def a1(t):
        slot=t%2
        full=rows_norm(feat[t].astype(F32))
        for l in range(C//128):
            normed[slot*(C//128)+l]=full[:,l*128:(l+1)*128]
        for l in range(C//128):
            held=slot*(C//128)+l
            for dy in range(2):
                for dx in range(2):
                    rows=[normed[held,pl.ds((2*i+dy)*2*side+dx,side,stride=2),:] for i in range(side)]
                    at=(dy*2+dx)*C+l*128
                    patches[t*S:(t+1)*S, at:at+128]=jnp.concatenate(rows,axis=0).astype(BF)
    def a2(c, w):
        red[:,c*w:(c+1)*w]=jnp.dot(patches[...],down[:,c*w:(c+1)*w],preferred_element_type=F32).astype(BF)
    def a3(t):
        f=jnp.dot(fwd[...],red[t*S:(t+FT)*S,:],preferred_element_type=F32)
        kr,ki=khat[:FREQ,:],khat[FREQ:,:]
        gs=[]
        for u in range(FT):
            fr,fi=f[2*u*FREQ:(2*u+1)*FREQ],f[(2*u+1)*FREQ:(2*u+2)*FREQ]
            pool[pl.ds(step*G+t+u,1),:]=fr[0:1]*(1.0/S)
            gs+=[(fr*kr-fi*ki).astype(BF),(fr*ki+fi*kr).astype(BF)]
        for u in range(0,FT,IT):
            g=jnp.concatenate(gs[2*u:2*(u+IT)],axis=0)
            sp=jnp.dot(inv[...],g,preferred_element_type=F32)
            sn_a[(t+u)*S:(t+u+IT)*S,:]=rows_norm(sp).astype(BF)
    def b1(c):
        hbuf[c%2]=jnp.dot(sn_b[...],win[:,c*NC:(c+1)*NC],preferred_element_type=F32).astype(hbuf.dtype)
    def b2(c):
        psum[pl.ds(pl.multiple_of((step-1)*G*8,G*8),G*8), c*NC:(c+1)*NC]=gelu_sums(hbuf[c%2],G,S).astype(BF)
    a_items=[(lambda t=t:a1(t)) for t in range(G)]+[(lambda c=c:a2(c,256)) for c in range(D//256)]+[(lambda t=t:a3(t)) for t in range(0,G,FT)]
    b_items=[]
    for c in range(M//NC+1):
        def item(c=c):
            if c<M//NC: b1(c)
            if c>0: b2(c-1)
        b_items.append(item)
    def keep():
        sn_b[...]=sn_a[...]

    @pl.when(step==0)
    def _():
        cp_down.start()
        for cp in cp_small: cp.start()
        cp_in.start(); cp_out.start()
        out[:,D:]=meta_cols(slides,places,T,blocks)
        for t in range(G): a1(t)
        for cp in cp_small: cp.wait()
        t2=jnp.dot(taptab[...],taps[...],preferred_element_type=F32)
        khat[...]=t2[:2*FREQ]+t2[2*FREQ:]
        cp_down.wait()
        for f in a_items[G:]: f()
        cp_in.wait()
        keep()
    @pl.when((step>0)&(step<steps))
    def _():
        na,nb=len(a_items),len(b_items)
        done=0
        for i,f in enumerate(b_items):
            f()
            upto=(i+1)*na//nb
            for g in a_items[done:upto]: g()
            done=upto
        keep()
    @pl.when(step==steps)
    def _():
        for f in b_items: f()
        cp_out.wait()
        z=jnp.dot(psum[...],wout[...],preferred_element_type=F32)
        z=z.reshape(z.shape[0]//8,8,D).sum(axis=1)*(0.5/S)
        out[:,:D]=rows_norm(pool[...]+scale[...].reshape(1,D)*z).astype(BF)

def encode(feature_maps, down, taps, win, wout, scale, tile_slide, tile_pos, G=8, NC=256, hb=BF):
    T,H,W,C=feature_maps.shape
    side=H//2; S=side*side; D=down.shape[1]; M=win.shape[1]; ks=int(round(taps.shape[0]**.5))
    fwd,inv,tt=tables(side,ks)
    blocks=lax.axis_size("ctx")
    steps=T//G


    fwd=np.kron(np.eye(FT),fwd); inv=np.kron(np.eye(IT),inv)
    full=lambda a: pl.BlockSpec(a.shape,lambda s:(0,)*a.ndim,pipeline_mode=pl.Buffered(1))
    hbm=pl.BlockSpec(memory_space=pltpu.HBM); smem=pl.BlockSpec(memory_space=pltpu.SMEM)
    held=[down,win,wout,taps]+[jnp.asarray(a,BF) for a in (fwd,inv,tt)]
    r=pl.pallas_call(
        functools.partial(kernel,G,side,blocks,NC,steps),
        grid=(steps+1,),
        in_specs=[pl.BlockSpec((G,H*W,C),lambda s:(jnp.minimum(s,steps-1),0,0))]+[hbm]*7+[full(scale),smem,smem],
        out_specs=pl.BlockSpec((T,D+META),lambda s:(0,0)),
        out_shape=pltpu.VMEM((T,D+META),BF),
        scratch_shapes=[pltpu.VMEM((G*S,4*C),BF),pltpu.VMEM((G*S,D),BF),pltpu.VMEM((G*S,D),BF),pltpu.VMEM((G*S,D),BF),
                        pltpu.VMEM((T*8,M),BF),pltpu.VMEM((T,D),F32),pltpu.VMEM((2*FREQ,D),F32),
                        pltpu.VMEM((2,G*S,NC),hb)]+[pltpu.VMEM(a.shape,BF) for a in held]+[pltpu.VMEM((2*(C//128),H*W,128),F32)]+[pltpu.SemaphoreType.DMA((len(held),))],
        compiler_params=pltpu.CompilerParams(vmem_limit_bytes=VM*1024*1024, dimension_semantics=("arbitrary",)),
        name="encode",
    )(feature_maps.reshape(T,H*W,C),*held,scale,tile_slide,tile_pos)
    return r


def gather_rows(rows, count):
    span_left = count
    while span_left > 1:
        span = 4 if span_left >= 4 else 2
        unit = span_left // span
        parts = [rows]
        for mask in range(1, span):
            pairs = [(dev, dev ^ (mask * unit)) for dev in range(count)]
            parts.append(lax.ppermute(rows, ("slide", "ctx"), pairs))
        span_left = unit
        if span_left > 1:
            rows = jnp.concatenate(parts, axis=0)
    return parts


def take_part(part, qkv, chunk, rows_dev, my_slide, my_ctx, keyvals):
    D = part.shape[1] - META
    pick_lane = (
        lax.broadcasted_iota(jnp.int32, (8, META), 0) == lax.broadcasted_iota(jnp.int32, (8, META), 1)
    ).astype(BF)
    ids = lax.dot_general(
        pick_lane, part[:, D:], (((1,), (1,)), ((), ())), preferred_element_type=F32
    )
    here = ids[0:1] == my_slide.astype(F32)
    target = jnp.where(here & (ids[1:2] == my_ctx.astype(F32)), ids[2:3], -1.0)
    slot = lax.broadcasted_iota(jnp.int32, (rows_dev, 1), 0).astype(F32)
    picking = (slot == target).astype(BF)
    for start in range(0, part.shape[0], chunk):
        rows = slice(start, start + chunk)
        lnorm = rows_norm(part[rows, :D].astype(F32)).astype(BF)
        keyvals[rows, :] = jnp.dot(lnorm, qkv[:, D:], preferred_element_type=F32).astype(BF)
    picked = jnp.dot(picking, part[:, :D], preferred_element_type=F32)
    return picked, here, ids[1:2] * float(rows_dev) + ids[2:3]


def project_kernel(chunk, part, qkv, keyvals, picked):
    my_slide, my_ctx = lax.axis_index("slide"), lax.axis_index("ctx")
    rows, _, _ = take_part(part, qkv, chunk, picked.shape[0], my_slide, my_ctx, keyvals)
    picked[...] = rows.astype(BF)


def attend_kernel(chunk, near, far, near_keyvals, near_picked, qkv, wout, lens, out, far_keyvals, attended):
    D = wout.shape[0]
    rows_dev = out.shape[0]
    my_slide, my_ctx = lax.axis_index("slide"), lax.axis_index("ctx")
    length = lens[my_slide].astype(F32)
    pick_lane = (
        lax.broadcasted_iota(jnp.int32, (8, META), 0) == lax.broadcasted_iota(jnp.int32, (8, META), 1)
    ).astype(BF)
    ids = lax.dot_general(
        pick_lane, near[:, D:], (((1,), (1,)), ((), ())), preferred_element_type=F32
    )
    near_here = ids[0:1] == my_slide.astype(F32)
    near_place = ids[1:2] * float(rows_dev) + ids[2:3]
    picked, far_here, far_place = take_part(far, qkv, chunk, rows_dev, my_slide, my_ctx, far_keyvals)
    here = jnp.concatenate([near_here, far_here], axis=1)
    place = jnp.concatenate([near_place, far_place], axis=1)
    bias = jnp.where(here & (place < length), 0.0, FAR_NEGATIVE)
    stream = near_picked[...].astype(F32) + picked
    lnorm = rows_norm(stream).astype(BF)
    queries = jnp.dot(lnorm, qkv[:, :D], preferred_element_type=F32).astype(BF)
    lane = lax.broadcasted_iota(jnp.int32, (1, 2 * HEAD_DIM), 1)
    low = lane < HEAD_DIM
    scale = jnp.asarray(HEAD_DIM**-0.5, BF)
    half = near.shape[0]
    ones = jnp.ones((half, 2 * HEAD_DIM), BF)
    for pair in range(HEADS // 2):
        cols = slice(pair * 2 * HEAD_DIM, (pair + 1) * 2 * HEAD_DIM)
        vcols = slice(D + pair * 2 * HEAD_DIM, D + (pair + 1) * 2 * HEAD_DIM)
        both = queries[:, cols] * scale
        zero = jnp.zeros_like(both)
        stacked = jnp.concatenate([jnp.where(low, both, zero), jnp.where(low, zero, both)], axis=0)
        scores = [
            lax.dot_general(stacked, held[:, cols], (((1,), (1,)), ((), ())), preferred_element_type=F32)
            for held in (near_keyvals, far_keyvals)
        ]
        scores = [scores[0] + bias[:, :half], scores[1] + bias[:, half:]]
        peak = jnp.max(jnp.maximum(scores[0], scores[1]), axis=-1, keepdims=True)
        mixed = jnp.zeros((2 * rows_dev, 4 * HEAD_DIM), F32)
        for part, held in zip(scores, (near_keyvals, far_keyvals)):
            values = jnp.concatenate([held[:, vcols], ones], axis=1)
            mixed = mixed + jnp.dot(jnp.exp((part - peak).astype(BF)), values, preferred_element_type=F32)
        mixed = mixed[:, : 2 * HEAD_DIM] / mixed[:, 2 * HEAD_DIM :]
        attended[:, cols] = jnp.where(low, mixed[:rows_dev], mixed[rows_dev:]).astype(BF)
    stream = stream + jnp.dot(attended[...], wout[...], preferred_element_type=F32)
    slot = lax.broadcasted_iota(jnp.int32, (rows_dev, 1), 0).astype(F32)
    valid = (slot + my_ctx.astype(F32) * float(rows_dev)) < length
    out[...] = jnp.where(valid, stream, 0.0).astype(BF)


VMEM_SPEC = pl.BlockSpec(memory_space=pltpu.VMEM)


def project(part, qkv):
    rows, width = part.shape
    D = width - META
    return pl.pallas_call(
        functools.partial(project_kernel, min(256, rows)),
        in_specs=[VMEM_SPEC] * 2,
        out_specs=[VMEM_SPEC] * 2,
        out_shape=[pltpu.VMEM((rows, 2 * D), BF), pltpu.VMEM((SEQ_DEV, D), BF)],
        compiler_params=pltpu.CompilerParams(vmem_limit_bytes=24 * 1024 * 1024),
        cost_estimate=pl.CostEstimate(flops=4 * rows * D * D, bytes_accessed=8 * rows * D, transcendentals=rows),
        name="project",
    )(part, qkv)


def attend(near, far, keyvals, picked, qkv, wout, lens):
    D = wout.shape[0]
    rows = far.shape[0]
    return pl.pallas_call(
        functools.partial(attend_kernel, min(256, rows)),
        in_specs=[VMEM_SPEC] * 6 + [pl.BlockSpec(memory_space=pltpu.SMEM)],
        out_specs=VMEM_SPEC,
        out_shape=jax.ShapeDtypeStruct((SEQ_DEV, D), BF),
        scratch_shapes=[pltpu.VMEM((rows, 2 * D), BF), pltpu.VMEM((SEQ_DEV, D), BF)],
        compiler_params=pltpu.CompilerParams(vmem_limit_bytes=24 * 1024 * 1024),
        name="attend",
    )(near, far, keyvals, picked, qkv, wout, lens)


def shards(
    feature_maps,
    down_weight,
    conv_taps,
    mlp_in,
    mlp_out,
    layer_scale,
    qkv_weight,
    out_weight,
    tile_slide,
    tile_pos,
    slide_len,
):
    device_count = lax.axis_size("slide") * lax.axis_size("ctx")
    rows = encode(
        feature_maps, down_weight, conv_taps, mlp_in, mlp_out, layer_scale, tile_slide, tile_pos
    )
    near, far = gather_rows(rows, device_count)
    keyvals, picked = project(near, qkv_weight[0])
    return attend(near, far, keyvals, picked, qkv_weight[0], out_weight[0], slide_len)


def solution(mesh):
    return jax.shard_map(
        shards,
        mesh=mesh,
        in_specs=(
            P(("slide", "ctx"), None, None, None),
            P(),
            P(),
            P(),
            P(),
            P(),
            P(),
            P(),
            P(("slide", "ctx")),
            P(("slide", "ctx")),
            P(),
        ),
        out_specs=P(("slide", "ctx"), None),
        check_vma=False,
    )
```

time: 71.5 us -> 61.8 us (0.86)
  Pallas kernels: 43.1 us -> 37.9 us
  waiting for transfers between devices: 16 us -> 14.1 us
  local copies, waits for them, and re-layouts: 1.96 us -> 0.14 us
  other arithmetic: 0.84 us -> 0.02 us
    pallas_call x1, Pallas kernels: 32 us -> 28.8 us  [encode(): pl.pallas_call(functools.partial(kernel, G, side, blocks, NC, steps), gri...]
    pallas_call x1 -> x2, Pallas kernels: 11.1 us -> 9.08 us  [the longest x1 7.25 us: attend(): pl.pallas_call(functools.partial(attend_kernel, min(256, rows)), in_specs...]
    ppermute x7, waiting for transfers between devices: 16 us -> 14.1 us  [gather_rows(): parts.append(lax.ppermute(rows, ('slide', 'ctx'), pairs))]
    unnamed x10 -> x12, local copies, waits for them, and re-layouts: 1.93 us -> 0.11 us
    concatenate x1, other arithmetic: 0.84 us -> 0.02 us  [gather_rows(): rows = jnp.concatenate(parts, axis=0)]
  transfers between devices with their start and end apart: 7 -> 7, of which waited for: 6 -> 5; matrix products, arithmetic and copies ran while one was open for 1% -> 0% of each run, Pallas kernels for 0% -> 3%
where the time goes in v3:
time: 61.8 us; the launch traced here: 61.6 us
  Pallas kernels  37.9 us (61%)
  waiting for transfers between devices  14.1 us (23%)
  starting transfers between devices  9.38 us (15%)
    pallas_call x1, Pallas kernels, encode(): pl.pallas_call(functools.partial(kernel, G, side, blocks, NC, steps), gri...  28.8 us
    ppermute x7, waiting for transfers between devices, gather_rows(): parts.append(lax.ppermute(rows, ('slide', 'ctx'), pairs))  14.1 us
    ppermute x7, starting transfers between devices, gather_rows(): parts.append(lax.ppermute(rows, ('slide', 'ctx'), pairs))  9.38 us
    pallas_call x1, Pallas kernels, attend(): pl.pallas_call(functools.partial(attend_kernel, min(256, rows)), in_specs...  7.25 us
    pallas_call x1, Pallas kernels, project(): pl.pallas_call(functools.partial(project_kernel, min(256, rows)), in_spec...  1.83 us
  transfers between devices with their start and end apart: 7, of which 5 were waited for; matrix products, arithmetic and copies ran while one was open for 0% of the time, Pallas kernels for 3%

profile of v3, /device:TPU:0, one launch (start us, length us, event | category | flops | bytes accessed | tf_op | source)
XLA Modules:
  0.0 61.6 jit_solution(1368217026328171581)
XLA Ops:
  0.0 0.0 copy-start
  0.0 28.8 %encode.1 = bf16[32,896]{1,0:T(8,128)(2,1)S(1)} custom-call(bf16[32,256,384]{2,1,0:T(8,128)(2,1)} %bitcast.6, bf16[1536,768]{1,0:T(8,128)(2,1)} %down_h.1, bf16[768,3072]{1,0:T(8,128)(2,1)} %win_h.1, bf16[3072,768]{1,0:T(8,128)(2,1)} %wout_h.1, bf16[49,768]{1,0:T(8,128)(2,1)} %taps_h.1, bf16[512,256]{1,0:T(8,128)(2,1)} %constant.6.clone.fwd_h, ...), custom_call_target="tpu_custom_call" | custom-call | tf_op jit(solution)/shard_map/encode/pallas_call | solution.py:163
  28.8 0.0 copy-start.1
  28.8 0.0 copy-start.2
  28.8 5.1 %collective-permute-start.2 = (bf16[32,896]{1,0:T(8,128)(2,1)S(1)}, bf16[32,896]{1,0:T(8,128)(2,1)S(1)}, u32[]{:S(2)}, u32[]{:S(2)}) collective-permute-start(bf16[32,896]{1,0:T(8,128)(2,1)S(1)} %encode.1), channel_id=1, source_target_pairs={{0,24},{1,25},{2,26},{3,27},{4,28},{5,29},{6,30},{7,31},{8,16},{9,... | collective-permute-start | bytes 172040 | tf_op jit(solution)/shard_map/ppermute | solution.py:186
  34.0 0.0 collective-permute-start.1
  34.0 0.6 %collective-permute-start = (bf16[32,896]{1,0:T(8,128)(2,1)S(1)}, bf16[32,896]{1,0:T(8,128)(2,1)S(1)}, u32[]{:S(2)}, u32[]{:S(2)}) collective-permute-start(bf16[32,896]{1,0:T(8,128)(2,1)S(1)} %encode.1), channel_id=1, source_target_pairs={{0,8},{1,9},{2,10},{3,11},{4,12},{5,13},{6,14},{7,15},{8,0},{9,1},... | collective-permute-start | bytes 172040 | tf_op jit(solution)/shard_map/ppermute | solution.py:186
  34.6 1.8 %collective-permute-done.2 = bf16[32,896]{1,0:T(8,128)(2,1)S(1)} collective-permute-done((bf16[32,896]{1,0:T(8,128)(2,1)S(1)}, bf16[32,896]{1,0:T(8,128)(2,1)S(1)}, u32[]{:S(2)}, u32[]{:S(2)}) %collective-permute-start.2) | collective-permute-done | bytes 57376 | tf_op jit(solution)/shard_map/ppermute | solution.py:186
  36.4 2.7 %collective-permute-done.1 = bf16[32,896]{1,0:T(8,128)(2,1)S(1)} collective-permute-done((bf16[32,896]{1,0:T(8,128)(2,1)S(1)}, bf16[32,896]{1,0:T(8,128)(2,1)S(1)}, u32[]{:S(2)}, u32[]{:S(2)}) %collective-permute-start.1) | collective-permute-done | bytes 57376 | tf_op jit(solution)/shard_map/ppermute | solution.py:186
  39.0 0.0 collective-permute-done
  39.1 2.5 %collective-permute-start.5 = (bf16[128,896]{1,0:T(8,128)(2,1)S(1)}, bf16[128,896]{1,0:T(8,128)(2,1)S(1)}, u32[]{:S(2)}, u32[]{:S(2)}) collective-permute-start(bf16[128,896]{1,0:T(8,128)(2,1)S(1)} %pad_maximum_fusion), channel_id=1, source_target_pairs={{0,6},{1,7},{2,4},{3,5},{4,2},{5,3},{6,0},{7,1},{8,14},{9,15},{10,... | collective-permute-start | bytes 688136 | tf_op jit(solution)/shard_map/ppermute | solution.py:186
  41.6 0.5 collective-permute-start.4
  42.1 0.5 collective-permute-start.3
  42.7 8.9 %collective-permute-done.3 = bf16[128,896]{1,0:T(8,128)(2,1)S(1)} collective-permute-done((bf16[128,896]{1,0:T(8,128)(2,1)S(1)}, bf16[128,896]{1,0:T(8,128)(2,1)S(1)}, u32[]{:S(2)}, u32[]{:S(2)}) %collective-permute-start.3) | collective-permute-done | bytes 229408 | tf_op jit(solution)/shard_map/ppermute | solution.py:186
  51.6 0.2 collective-permute-done.4
  51.8 0.0 collective-permute-done.5
  51.8 0.1 collective-permute-start.6
  51.9 0.0 copy-done
  51.9 1.8 %project.1 = (bf16[512,1536]{1,0:T(8,128)(2,1)S(1)}, bf16[192,768]{1,0:T(8,128)(2,1)S(1)}) custom-call(bf16[512,896]{1,0:T(8,128)(2,1)S(1)} %constant_dynamic-update-slice_fusion.part.near, bf16[768,2304]{1,0:T(8,128)(2,1)S(1)} %bitcast.3), custom_call_target="tpu_custom_call" | custom-call | flops 1207959552 | bytes 3145728 | tf_op jit(solution)/shard_map/project/pallas_call | solution.py:274
  53.8 0.6 collective-permute-done.6.far
  54.4 0.0 copy-done.1
  54.4 0.0 copy-done.2
  54.4 7.2 %attend.1 = bf16[192,768]{1,0:T(8,128)(2,1)} custom-call(bf16[512,896]{1,0:T(8,128)(2,1)S(1)} %constant_dynamic-update-slice_fusion.part.near, bf16[512,896]{1,0:T(8,128)(2,1)S(1)} %collective-permute-done.6.far, bf16[512,1536]{1,0:T(8,128)(2,1)S(1)} %get-tuple-element.7.near_keyvals, bf16[192,768]{1,0:T(8,128)(2,1)S(1)} %get-tuple-element.8.near_picked, ...), custom_call_target="tpu_custom_call" | custom-call | tf_op jit(solution)/shard_map/attend/pallas_call | solution.py:288
  (8 shorter events, 0.1 us)
Async XLA Ops:
  0.0 51.9 %copy-start = (bf16[1,768,2304]{2,1,0:T(8,128)(2,1)S(1)}, bf16[1,768,2304]{2,1,0:T(8,128)(2,1)}, u32[]{:S(2)}) copy-start(bf16[1,768,2304]{2,1,0:T(8,128)(2,1)} %param.20) | copy-start | bytes 10616836
  28.8 25.6 %copy-start.1 = (bf16[1,768,768]{2,1,0:T(8,128)(2,1)S(1)}, bf16[1,768,768]{2,1,0:T(8,128)(2,1)}, u32[]{:S(2)}) copy-start(bf16[1,768,768]{2,1,0:T(8,128)(2,1)} %param.21) | copy-start | bytes 3538948
  28.8 25.6 %copy-start.2 = (s32[8]{0:T(128)S(1)}, s32[8]{0:T(128)}, u32[]{:S(2)}) copy-start(s32[8]{0:T(128)} %lens.1) | copy-start | bytes 100
  28.8 7.5 %collective-permute-start.2 = (bf16[32,896]{1,0:T(8,128)(2,1)S(1)}, bf16[32,896]{1,0:T(8,128)(2,1)S(1)}, u32[]{:S(2)}, u32[]{:S(2)}) collective-permute-start(bf16[32,896]{1,0:T(8,128)(2,1)S(1)} %encode.1), channel_id=1, source_target_pairs={{0,24},{1,25},{2,26},{3,27},{4,28},{5,29},{6,30},{7,31},{8,16},{9,... | collective-permute-start | bytes 172040 | tf_op jit(solution)/shard_map/ppermute | solution.py:186
  34.0 5.1 %collective-permute-start.1 = (bf16[32,896]{1,0:T(8,128)(2,1)S(1)}, bf16[32,896]{1,0:T(8,128)(2,1)S(1)}, u32[]{:S(2)}, u32[]{:S(2)}) collective-permute-start(bf16[32,896]{1,0:T(8,128)(2,1)S(1)} %encode.1), channel_id=1, source_target_pairs={{0,16},{1,17},{2,18},{3,19},{4,20},{5,21},{6,22},{7,23},{8,24},{9,... | collective-permute-start | bytes 172040 | tf_op jit(solution)/shard_map/ppermute | solution.py:186
  34.0 5.1 %collective-permute-start = (bf16[32,896]{1,0:T(8,128)(2,1)S(1)}, bf16[32,896]{1,0:T(8,128)(2,1)S(1)}, u32[]{:S(2)}, u32[]{:S(2)}) collective-permute-start(bf16[32,896]{1,0:T(8,128)(2,1)S(1)} %encode.1), channel_id=1, source_target_pairs={{0,8},{1,9},{2,10},{3,11},{4,12},{5,13},{6,14},{7,15},{8,0},{9,1},... | collective-permute-start | bytes 172040 | tf_op jit(solution)/shard_map/ppermute | solution.py:186
  39.1 12.7 %collective-permute-start.5 = (bf16[128,896]{1,0:T(8,128)(2,1)S(1)}, bf16[128,896]{1,0:T(8,128)(2,1)S(1)}, u32[]{:S(2)}, u32[]{:S(2)}) collective-permute-start(bf16[128,896]{1,0:T(8,128)(2,1)S(1)} %pad_maximum_fusion), channel_id=1, source_target_pairs={{0,6},{1,7},{2,4},{3,5},{4,2},{5,3},{6,0},{7,1},{8,14},{9,15},{10,... | collective-permute-start | bytes 688136 | tf_op jit(solution)/shard_map/ppermute | solution.py:186
  41.6 10.2 %collective-permute-start.4 = (bf16[128,896]{1,0:T(8,128)(2,1)S(1)}, bf16[128,896]{1,0:T(8,128)(2,1)S(1)}, u32[]{:S(2)}, u32[]{:S(2)}) collective-permute-start(bf16[128,896]{1,0:T(8,128)(2,1)S(1)} %pad_maximum_fusion), channel_id=1, source_target_pairs={{0,4},{1,5},{2,6},{3,7},{4,0},{5,1},{6,2},{7,3},{8,12},{9,13},{10,... | collective-permute-start | bytes 688136 | tf_op jit(solution)/shard_map/ppermute | solution.py:186
  42.1 9.4 %collective-permute-start.3 = (bf16[128,896]{1,0:T(8,128)(2,1)S(1)}, bf16[128,896]{1,0:T(8,128)(2,1)S(1)}, u32[]{:S(2)}, u32[]{:S(2)}) collective-permute-start(bf16[128,896]{1,0:T(8,128)(2,1)S(1)} %pad_maximum_fusion), channel_id=1, source_target_pairs={{0,2},{1,3},{2,0},{3,1},{4,6},{5,7},{6,4},{7,5},{8,10},{9,11},{10,... | collective-permute-start | bytes 688136 | tf_op jit(solution)/shard_map/ppermute | solution.py:186
  51.8 2.5 %collective-permute-start.6 = (bf16[512,896]{1,0:T(8,128)(2,1)S(1)}, bf16[512,896]{1,0:T(8,128)(2,1)S(1)}, u32[]{:S(2)}, u32[]{:S(2)}) collective-permute-start(bf16[512,896]{1,0:T(8,128)(2,1)S(1)} %constant_dynamic-update-slice_fusion.part.near), channel_id=1, source_target_pairs={{0,1},{1,0},{2,3},{3,2},{4,5},{5,4},{6,7},{7,6},{8,9},{9,8},{10,11... | collective-permute-start | bytes 2752520 | tf_op jit(solution)/shard_map/ppermute | solution.py:186
